TPU v7x, 32 devices: a whole 2x2x4 slice. The times are simulated.
32 devices in a mesh: dp: 8 (over z, x), inner: 4 (over y, core).
Axes of the slice: x: 2, y: 2, z: 4, core: 2. Of those that a mesh axis runs over, the one named last changes fastest.
Arguments:
- hidden: float32 [65536, 253], P(('dp', 'inner')), may hold values from -6 to 6
- codes: float32 [16, 256], replicated, may hold values from -40 to 40, as said below
- offsets: float32 [65536, 3], P(('dp', 'inner')), may hold values from -6 to 6
- shape_ids: int32 [65536], P(('dp', 'inner')), may hold values from 0 to 15, as said below
- scale_index: int32 [65536], P(('dp', 'inner')), may hold values from 0 to 2, as said below
- direction: float32 [512, 512], P(('dp', 'inner')), may hold values from -0.25 to 0.25
- gain: float32 [512], P(('dp', 'inner')), may hold values from 0.5 to 2
- bias: float32 [512], P(('dp', 'inner')), may hold values from -3 to 3
- cotangent: float32 [65536, 512], P(('dp', 'inner')), may hold values from -6 to 6
- running_mean: float32 [256], replicated, may hold values from -3 to 3
- running_var: float32 [256], replicated, may hold values from 0.5 to 2
Outputs:
- output: float32 [65536, 512], P(('dp', 'inner'))
- grad_hidden: float32 [65536, 253], P(('dp', 'inner'))
- grad_codes: float32 [16, 256], replicated
- grad_direction: float32 [512, 512], P(('dp', 'inner'))
- grad_gain: float32 [512], P(('dp', 'inner'))
- grad_bias: float32 [512], P(('dp', 'inner'))
- new_mean: float32 [256], replicated
- new_var: float32 [256], replicated
Inputs may be any that keep to these rules, and one draw needn't show every extreme that they name: codes have row scales that differ between shapes. `shape_ids`: each shape has exactly 4096 points. `scale_index`: over all points exactly 32768 have index 0 and 20480 have index 1.
All inputs are finite; a program needn't handle non-finite values.
Results may differ from a plain program's by a relative error of at most 0.0067.
Values may be sent and summed in bfloat16 or wider, within the bound.
No kernel may reach another device: no remote copies, remote signals or barrier semaphores. Data moves between devices by JAX's collectives and lax.ppermute only.
A program may use at most 64 MiB of HBM per device.

v0:
```python
import functools

import jax
import jax.numpy as jnp
from jax import lax
from jax.experimental import pallas as pl
from jax.experimental.pallas import tpu as pltpu
from jax.sharding import PartitionSpec as P

AXES = ("dp", "inner")
LANES = 128
MIB = 1024 * 1024
FIRST = (2, 3, 1, 0)
SUMS = (1, 3, 2, 0)
F32 = jnp.float32
BF16 = jnp.bfloat16
VMEM = pltpu.VMEM
NT = (((1,), (1,)), ((), ()))


def dot(a, b, dims=(((1,), (0,)), ((), ()))):
    return lax.dot_general(a, b, dims, preferred_element_type=F32)


def vmem(n):
    return [pl.BlockSpec(memory_space=VMEM)] * n


def small_kernel(name, body, out_shape, *args, scratch=(), space=VMEM, limit=8):
    many = isinstance(out_shape, list)
    return pl.pallas_call(
        body,
        out_shape=out_shape,
        in_specs=[pl.BlockSpec(memory_space=space)] * len(args),
        out_specs=vmem(len(out_shape)) if many else vmem(1)[0],
        scratch_shapes=list(scratch),
        compiler_params=pltpu.CompilerParams(vmem_limit_bytes=limit * MIB),
        cost_estimate=pl.CostEstimate(
            flops=4000 * MIB, bytes_accessed=8 * MIB, transcendentals=4 * MIB
        ),
        name=name,
    )(*args)


def diagonal(n):
    return lax.broadcasted_iota(jnp.int32, (n, n), 0) == lax.broadcasted_iota(jnp.int32, (n, n), 1)


def to_column(row):
    n = row.shape[1]
    return jnp.sum(jnp.where(diagonal(n), row, 0.0), axis=1, keepdims=True)


def to_row(column):
    n = column.shape[0]
    return jnp.sum(jnp.where(diagonal(n), column, 0.0), axis=0, keepdims=True)


def stacked_codes(codes_ref, count):
    codes = codes_ref[...].astype(BF16)
    parts = [codes, codes]
    if count > 2 * codes.shape[0]:
        parts.append(jnp.zeros((count - 2 * codes.shape[0], codes.shape[1]), BF16))
    return jnp.concatenate(parts, axis=0)


def split(x):
    high = x.astype(BF16).astype(F32)
    return high, x - high


def prep_kernel(hid, *refs):
    piece_ref, direction_ref, gain_ref, bias_ref, codes_ref, sems = refs[4:]
    copies = [
        pltpu.make_async_copy(source, target, sems.at[k])
        for k, (source, target) in enumerate(zip(refs[:4], refs[5:9]))
    ]
    for copy in copies:
        copy.start()
    for copy in copies:
        copy.wait()
    d = direction_ref[...]
    shapes = codes_ref.shape[0]
    rows, cols = d.shape
    half = cols // 2
    extra_lanes = piece_ref.shape[1] - cols
    inverse = lax.rsqrt(jnp.sum(d * d, axis=1, keepdims=True))
    w = to_column(gain_ref[...]) * (d * inverse)
    lane = lax.broadcasted_iota(jnp.int32, (rows, half), 1)
    first = jnp.where(lane < hid, w[:, :half], w[:, half:])
    code = pltpu.roll(w, half - hid, 1)[:, half:].astype(BF16)
    bias = to_column(bias_ref[...]).astype(BF16).astype(F32)
    high, low = split(dot(code, stacked_codes(codes_ref, extra_lanes), NT) + bias)
    own = first[:, half - LANES :]
    if extra_lanes > LANES:
        own = jnp.concatenate([jnp.zeros((rows, extra_lanes - LANES), F32), own], axis=1)
    lane = lax.broadcasted_iota(jnp.int32, (rows, extra_lanes), 1)
    table = jnp.where(lane < shapes, high, jnp.where(lane < 2 * shapes, low, 0.0))
    table = jnp.where(lane >= extra_lanes - (half - hid), own, table)
    piece_ref[:, :half] = first.astype(BF16)
    piece_ref[:, half : half + extra_lanes] = table.astype(BF16)
    piece_ref[:, half + extra_lanes :] = code


def join_kernel(n, n_early, *refs):
    rows = refs[0].shape[0]
    for k, ref in enumerate(refs[n - 1 :: -1]):
        lane = 0
        for out_ref in refs[n + n_early :]:
            lanes = out_ref.shape[1]
            out_ref[k * rows : (k + 1) * rows, :] = ref[:, lane : lane + lanes]
            lane += lanes


def pack_kernel(shapes, *refs):
    weight_ref, code_ref = refs[-2:]
    count = len(refs) - 2
    rows, half = refs[0].shape[0], code_ref.shape[1]
    products = jnp.zeros((rows, LANES), F32)
    for k, ref in zip(FIRST, refs):
        for block in range(half // LANES):
            at = (block * count + k) * rows
            weight_ref[at : at + rows, :] = ref[:, block * LANES : (block + 1) * LANES]
        own = ref[:, half : half + LANES].astype(F32)
        own = jnp.where(lax.broadcasted_iota(jnp.int32, own.shape, 1) < 2 * shapes, own, 0.0)
        products = products + (pltpu.roll(own, 2 * shapes * k, 1) if k else own)
        code_ref[k * rows : (k + 1) * rows, :] = ref[:, half + LANES :]
    weight_ref[half // LANES * count * rows :, :] = products.astype(BF16)


def unpack(hid, shapes, refs, orders, me, w_ref):
    count = LANES // (2 * shapes)
    half = w_ref.shape[1] - LANES
    blocks = half // LANES
    for ref, order in zip(refs, orders):
        height = ref.shape[0] // (len(order) // count)
        rows = height // (blocks * count + 1)
        lane = lax.broadcasted_iota(jnp.int32, (rows, LANES), 1)
        for j, mask in enumerate(order):
            start, k = j // count * height, j % count
            at = pl.ds(pl.multiple_of((me ^ mask) * rows, rows), rows)
            for block in range(blocks):
                here = start + (block * count + k) * rows
                part = ref[here : here + rows, :]
                w_ref[at, block * LANES : (block + 1) * LANES] = part
            here = start + blocks * count * rows
            products = ref[here : here + rows, :].astype(F32)
            if k:
                products = pltpu.roll(products, LANES - 2 * shapes * k, 1)
            products = jnp.where(lane < 2 * shapes, products, 0.0)
            products = jnp.where(lane >= LANES - (half - hid), part.astype(F32), products)
            w_ref[at, half:] = products.astype(BF16)


def place(refs, orders, me, out_ref):
    if orders is None:
        out_ref[...] = refs[0][...]
        return
    rows = refs[0].shape[0] // len(orders[0])
    for ref, order in zip(refs, orders):
        for k, mask in enumerate(order):
            at = pl.multiple_of((me ^ mask) * rows, rows)
            out_ref[pl.ds(at, rows), :] = ref[k * rows : (k + 1) * rows, :]


def inputs_kernel(hid, tile, *refs):
    x_ref, x_t_ref, hidden_ref, offsets_ref, ids_ref, scale_ref, sems = refs[4:]
    points = x_ref.shape[0]
    half = (hid + LANES - 1) // LANES * LANES
    shapes = x_t_ref.shape[0] - half
    extra_lanes = x_ref.shape[1] - half
    steps = points // tile
    small = [
        pltpu.make_async_copy(source, target, sems.at[steps + k])
        for k, (source, target) in enumerate(zip(refs[1:4], (offsets_ref, ids_ref, scale_ref)))
    ]
    large = [
        pltpu.make_async_copy(
            refs[0].at[pl.ds(k * tile, tile), :], hidden_ref.at[pl.ds(k * tile, tile), :], sems.at[k]
        )
        for k in range(steps)
    ]
    for copy in small + large:
        copy.start()
    for copy in small:
        copy.wait()
    for step, copy in enumerate(large):
        here = slice(step * tile, (step + 1) * tile)
        scale = scale_ref[:, here]
        jitter = jnp.where(scale == 0, 1.0, jnp.where(scale == 1, 0.5, 0.25))
        xyz = offsets_ref[:, here] * jitter
        row = lax.broadcasted_iota(jnp.int32, (16, tile), 0)
        last = jnp.zeros((16, tile), F32)
        for k in range(half - hid):
            last = jnp.where(row == 16 - (half - hid) + k, xyz[k : k + 1], last)
        last = last.astype(BF16)
        row = lax.broadcasted_iota(jnp.int32, (extra_lanes - 16, tile), 0)
        ids = ids_ref[:, here]
        member = jnp.where((row == ids) | (row == ids + shapes), 1.0, 0.0).astype(BF16)
        x_ref[here, half:] = jnp.concatenate([member, last], axis=0).T
        x_t_ref[half:, here] = member[:shapes]
        copy.wait()
        x_ref[here, half - LANES : half] = jnp.zeros((tile, LANES), BF16)
        x_ref[here, :hid] = hidden_ref[here, :].astype(BF16)
        hidden = x_ref[here, :half].T
        x_t_ref[: half - 16, here] = hidden[: half - 16]
        x_t_ref[half - 16 : half, here] = hidden[half - 16 :] + last


def layer_kernel(hid, shapes, tile, orders, parts, *refs):
    n = 1 if orders is None else len(orders)
    pieces = refs[:n]
    x_ref, x_t_ref, cot_ref, out_hbm, tail_ref, grad_hidden_ref = refs[n : n + 6]
    grad_refs = refs[n + 6 : -6]
    w_ref, turned_ref, out_ref, grad_pre_ref, pre_ref, sems = refs[-6:]
    points, width = cot_ref.shape
    half = width // 2
    steps = points // tile
    head = out_ref.shape[0] // tile
    me = lax.axis_index(AXES)
    if orders is None:
        place(pieces, orders, me, w_ref)
    else:
        unpack(hid, shapes, pieces, orders, me, w_ref)
    copies = []

    def rows_of(step):
        return slice(step * tile, (step + 1) * tile)

    def forward(step):
        pre_ref[step % 2] = dot(x_ref[rows_of(step), :], w_ref[...], NT)

    def middle(step):
        here = rows_of(step)
        pre = pre_ref[step % 2]
        sigma = 0.5 * jnp.tanh(0.5 * pre) + 0.5
        out = pre * sigma
        if step < head:
            out_ref[here, :] = out
        else:
            tail_ref[rows_of(step - head), :] = out
        grad_pre_ref[here, :] = (cot_ref[here, :] * (sigma * (1.0 + (pre - out)))).astype(BF16)

    def backward(step):
        here = rows_of(step)
        grad_hidden_ref[here, :] = dot(grad_pre_ref[here, :], w_ref[:, :half])[:, :hid]

    def store(step):
        here = pl.ds(step * tile, tile)
        copy = pltpu.make_async_copy(out_ref.at[here, :], out_hbm.at[here, :], sems.at[step])
        copy.start()
        copies.append(copy)

    forward(0)
    for step in range(steps):
        if step + 1 < steps:
            forward(step + 1)
        middle(step)
        if step > 0:
            backward(step - 1)
        if step < head:
            store(step)
    backward(steps - 1)
    grad = dot(x_t_ref[...], grad_pre_ref[...])
    sums = grad[half:].astype(BF16)
    for at in range(0, width, half):
        turned_ref[at : at + half, :] = grad[:half, at : at + half].T
    for ref, order in zip(grad_refs, parts):
        ref[:shapes, :] = sums[:, :half]
        ref[shapes : 2 * shapes, :] = sums[:, half:]
        if orders is None:
            ref[2 * shapes :, :] = turned_ref[...].astype(BF16)
            continue
        rows = (ref.shape[0] - 2 * shapes) // len(order)
        for k, mask in enumerate(order):
            at = pl.multiple_of((me ^ mask) * rows, rows)
            to = 2 * shapes + k * rows
            ref[to : to + rows, :] = turned_ref[pl.ds(at, rows), :].astype(BF16)

    for copy in copies:
        copy.wait()


def store_kernel(source_ref, target_ref, sem):
    copy = pltpu.make_async_copy(source_ref, target_ref, sem)
    copy.start()
    copy.wait()


def tail_kernel(_, source_ref, target_ref, sem):
    points, rows = target_ref.shape[0], source_ref.shape[0]
    store_kernel(source_ref, target_ref.at[pl.ds(points - rows, rows), :], sem)


def sum_of(refs):
    terms = [ref[...].astype(F32) for ref in refs]
    while len(terms) > 1:
        terms = [a + b for a, b in zip(terms[::2], terms[1::2])]
    return terms[0]


def add_kernel(shapes, n, *refs):
    total = sum_of(refs[:n]).astype(BF16)
    for k, ref in enumerate(refs[n:]):
        rows = ref.shape[0] - 2 * shapes
        at = 2 * shapes + k * rows
        ref[: 2 * shapes, :] = total[: 2 * shapes]
        ref[2 * shapes :, :] = total[at : at + rows]


def last_kernel(hid, shapes, orders, n, *refs):
    direction_ref, gain_ref, codes_ref = refs[n : n + 3]
    pieces = refs[n + 3 : -5]
    grad_codes_ref, grad_direction_ref, grad_gain_ref, grad_bias_ref, code_scratch = refs[-5:]
    d = direction_ref[...]
    rows, cols = d.shape
    half = cols // 2
    me = lax.axis_index(AXES)
    place(pieces, orders, me, code_scratch)
    total = sum_of(refs[:n])
    sums = jnp.concatenate([total[:shapes], total[shapes : 2 * shapes]], axis=1)
    sums = jnp.concatenate(split(sums), axis=0).astype(BF16)
    terms = dot(sums, code_scratch[...])
    grad_codes_ref[...] = terms[:shapes] + terms[shapes:]
    width = sums.shape[1]
    mine = lax.broadcasted_iota(jnp.int32, (rows, width), 0) + me * rows
    mine = jnp.where(mine == lax.broadcasted_iota(jnp.int32, (rows, width), 1), 1.0, 0.0).astype(BF16)
    own = dot(mine, sums, NT)
    grad_bias_ref[...] = to_row(jnp.sum(own, axis=1, keepdims=True))
    code = dot(own.astype(BF16), stacked_codes(codes_ref, 2 * shapes))
    packed = jnp.concatenate([total[2 * shapes :], code], axis=1)
    lane = lax.broadcasted_iota(jnp.int32, (rows, cols), 1)
    grad_weight = jnp.where(
        lane < hid,
        packed,
        jnp.where(lane < hid + half, pltpu.roll(packed, cols - (half - hid), 1), pltpu.roll(packed, half, 1)),
    )
    inverse = lax.rsqrt(jnp.sum(d * d, axis=1, keepdims=True))
    unit = d * inverse
    grad_gain = jnp.sum(grad_weight * unit, axis=1, keepdims=True)
    grad_gain_ref[...] = to_row(grad_gain)
    grad_direction_ref[...] = (to_column(gain_ref[...]) * inverse) * (grad_weight - grad_gain * unit)


def masks_of(group):
    masks = [0]
    for bit in group:
        masks = masks + [m ^ bit for m in masks]
    return masks


def order_of(groups):
    order = [0]
    for group in groups:
        order = [m ^ r for m in masks_of(group) for r in order]
    return order


def swaps(arrays, masks, devices):
    moved = [
        lax.ppermute(x, AXES, [(i, i ^ mask) for i in range(devices)])
        for x, mask in list(zip(arrays, masks))[::-1]
    ]
    return moved[::-1]


def per_device(
    hidden,
    codes,
    offsets,
    shape_ids,
    scale_index,
    direction,
    gain,
    bias,
    cotangent,
    running_mean,
    running_var,
):
    points, hid = hidden.shape
    shapes = codes.shape[0]
    rows, cols = direction.shape
    width = cotangent.shape[1]
    half = cols // 2
    devices = lax.axis_size("dp") * lax.axis_size("inner")
    bits = [1 << k | 1 for k in range(devices.bit_length() - 1)]
    groups = [bits[k - 2 : k] for k in range(len(bits), 1, -2)]
    groups = groups + [bits[:1]] * (len(bits) % 2)
    groups[0] = [groups[0][0], groups[0][-1] ^ 1]
    extra_lanes = -(-(2 * shapes + 16) // LANES) * LANES
    tuned = len(groups) == 3 and rows % 16 == 0 and 2 * shapes * len(masks_of(groups[0])) == LANES
    lanes = half + extra_lanes
    gain_row = gain.reshape(1, rows)

    def shape_of(rows, lanes, dtype):
        return jax.ShapeDtypeStruct((rows, lanes), dtype)

    held = small_kernel(
        "prep",
        functools.partial(prep_kernel, hid),
        shape_of(rows, lanes + half, BF16),
        *[
            pltpu.with_memory_space_constraint(x, pltpu.HBM)
            for x in (direction, gain_row, bias.reshape(1, rows), codes)
        ],
        scratch=[
            VMEM((rows, cols), F32),
            VMEM((1, rows), F32),
            VMEM((1, rows), F32),
            VMEM((shapes, half), F32),
            pltpu.SemaphoreType.DMA((4,)),
        ],
        space=pl.ANY,
    )
    tile, layer_tile = min(512, points), min(512, points)
    x, x_t = pl.pallas_call(
        functools.partial(inputs_kernel, hid, tile),
        out_shape=[
            shape_of(points, lanes, BF16),
            shape_of(half + shapes, points, BF16),
        ],
        in_specs=[pl.BlockSpec(memory_space=pl.ANY)] * 4,
        out_specs=vmem(2),
        scratch_shapes=[
            VMEM((points, hid), F32),
            VMEM((half - hid, points), F32),
            VMEM((1, points), jnp.int32),
            VMEM((1, points), jnp.int32),
            pltpu.SemaphoreType.DMA((points // tile + 3,)),
        ],
        compiler_params=pltpu.CompilerParams(vmem_limit_bytes=12 * MIB),
        cost_estimate=pl.CostEstimate(
            flops=4000 * MIB, bytes_accessed=8 * points * half, transcendentals=0
        ),
        name="inputs",
    )(
        *[
            pltpu.with_memory_space_constraint(a, pltpu.HBM)
            for a in (
                hidden,
                offsets.T,
                shape_ids.reshape(1, points),
                scale_index.reshape(1, points),
            )
        ]
    )
    def gather(array, group):
        masks = masks_of(group)[1:]
        return [array] + swaps([array] * len(masks), masks, devices)

    def join(arrays, *widths, early=()):
        height = sum(a.shape[0] for a in arrays)
        return small_kernel(
            "join",
            functools.partial(join_kernel, len(arrays), len(early)),
            [shape_of(height, width, BF16) for width in widths],
            *arrays[::-1],
            *early,
        )

    if tuned:
        arrays = gather(held, groups[0])
        weight, code_weight = small_kernel(
            "pack",
            functools.partial(pack_kernel, shapes),
            [
                shape_of((half // LANES * len(arrays) + 1) * rows, LANES, BF16),
                shape_of(len(arrays) * rows, half, BF16),
            ],
            *[arrays[k] for k in FIRST],
        )
        weight, code_weight, x, x_t = lax.optimization_barrier((weight, code_weight, x, x_t))
        (weights,) = [gather(weight, group) for group in groups[1:-1]]
        along, across = [[bit] for bit in groups[1][::-1]]
        (weight,) = join(weights, LANES, early=(cotangent,))
        weights = gather(weight, groups[-1])
        code_weights = gather(code_weight, along)
        code_order = order_of([groups[0], along, across])
        orders = [[m ^ r for r in order_of(groups[:-1])] for m in masks_of(groups[-1])]
        code_orders = [[m ^ r for r in code_order] for m in masks_of(groups[-1])]
        parts = orders
    else:
        held = lax.all_gather(held, AXES, axis=0, tiled=True)
        weights, code_weights, orders, code_orders, parts = [held[:, :lanes]], [held[:, lanes:]], None, None, [[0]]

    head = points // layer_tile // 2 * layer_tile
    output, tail, grad_hidden, *grads = pl.pallas_call(
        functools.partial(layer_kernel, hid, shapes, layer_tile, orders, parts),
        out_shape=[
            pltpu.HBM((points, width), F32),
            pltpu.VMEM((points - head, width), F32),
            pltpu.VMEM((points, hid), F32),
        ]
        + [shape_of(2 * shapes + width // len(parts), half, BF16)] * len(parts),
        in_specs=vmem(len(weights) + 3),
        out_specs=[pl.BlockSpec(memory_space=pltpu.HBM)] + vmem(2 + len(parts)),
        scratch_shapes=[
            VMEM((width, lanes), BF16),
            VMEM((width, half), F32),
            VMEM((head, width), F32),
            VMEM((points, width), BF16),
            VMEM((2, layer_tile, width), F32),
            pltpu.SemaphoreType.DMA((head // layer_tile,)),
        ],
        compiler_params=pltpu.CompilerParams(vmem_limit_bytes=20 * MIB),
        cost_estimate=pl.CostEstimate(
            flops=6 * points * width * cols,
            bytes_accessed=8 * points * (width + half),
            transcendentals=points * width,
        ),
        name="layer",
    )(*weights, x, x_t, cotangent)

    def store(name, body, shape, *args, **options):
        return pl.pallas_call(
            body,
            out_shape=pltpu.HBM(shape, F32),
            in_specs=[pl.BlockSpec(memory_space=pltpu.HBM)] * (len(args) - 1) + vmem(1),
            out_specs=pl.BlockSpec(memory_space=pltpu.HBM),
            scratch_shapes=[pltpu.SemaphoreType.DMA(())],
            compiler_params=pltpu.CompilerParams(vmem_limit_bytes=8 * MIB),
            cost_estimate=pl.CostEstimate(
                flops=4000 * MIB, bytes_accessed=8 * points * hid, transcendentals=0
            ),
            name=name,
            **options,
        )(*args)

    def store_grad_hidden():
        return store("store", store_kernel, (points, hid), grad_hidden)

    def store_tail():
        return store(
            "tail", tail_kernel, (points, width), output, tail, input_output_aliases={0: 0}
        )

    if tuned:
        *grads, code_along, running_mean, running_var = lax.optimization_barrier(
            (*grads, code_weights[1], running_mean, running_var)
        )
        (code_weight,) = join([code_weights[0], code_along], half)
        for r, group in enumerate(groups[::-1]):
            masks = masks_of(group)
            grads = [grads[0]] + swaps(grads[1:], masks[1:], devices)
            if r == len(groups) - 1:
                break
            n_out = len(masks_of(groups[-2 - r]))
            left = (grads[0].shape[0] - 2 * shapes) // n_out
            grads = small_kernel(
                "add",
                functools.partial(add_kernel, shapes, len(grads)),
                [shape_of(2 * shapes + left, half, BF16)] * n_out,
                *(grads[::-1] if r == 0 else [grads[k] for k in SUMS]),
            )
            if r == 0:
                *grads, grad_hidden = lax.optimization_barrier((*grads, grad_hidden))
                grad_hidden = store_grad_hidden()
                grad_hidden, code_weight = lax.optimization_barrier((grad_hidden, code_weight))
                code_weights = gather(code_weight, across)
            if r == len(groups) - 2:
                *grads, grad_hidden, tail = lax.optimization_barrier((*grads, grad_hidden, tail))
                output = store_tail()
        (code_weight,) = join(code_weights, half)
        code_weights = gather(code_weight, groups[-1])
    else:
        grad_hidden, output = store_grad_hidden(), store_tail()
        sums = lax.psum(grads[0][: 2 * shapes].astype(F32), AXES)
        high = sums.astype(BF16)
        own = lax.psum_scatter(grads[0][2 * shapes :].astype(F32), AXES, scatter_dimension=0, tiled=True)
        low = jnp.zeros((2 * shapes + rows, half), BF16).at[: 2 * shapes].set((sums - high).astype(BF16))
        grads = [jnp.concatenate([high, own.astype(BF16)], axis=0), low]
    grad_codes, grad_direction, grad_gain, grad_bias = small_kernel(
        "last",
        functools.partial(last_kernel, hid, shapes, code_orders, len(grads)),
        [
            shape_of(shapes, half, F32),
            shape_of(rows, cols, F32),
            shape_of(1, rows, F32),
            shape_of(1, rows, F32),
        ],
        *([grads[k] for k in FIRST] if tuned else grads),
        direction,
        gain_row,
        codes,
        *code_weights,
        scratch=[VMEM((width, half), BF16)],
    )

    total = float(points * devices)
    batch_mean = jnp.mean(codes, axis=0)
    batch_square = jnp.mean(codes * codes, axis=0)
    batch_var = (batch_square - batch_mean * batch_mean) * (total / (total - 1.0))
    new_mean = 0.9 * running_mean + 0.1 * batch_mean
    new_var = 0.9 * running_var + 0.1 * batch_var
    return (
        output,
        grad_hidden,
        grad_codes,
        grad_direction,
        grad_gain.reshape(rows),
        grad_bias.reshape(rows),
        new_mean,
        new_var,
    )


def solution(mesh):
    return jax.shard_map(
        per_device,
        mesh=mesh,
        in_specs=(
            P(("dp", "inner"), None),
            P(),
            P(("dp", "inner"), None),
            P(("dp", "inner")),
            P(("dp", "inner")),
            P(("dp", "inner"), None),
            P(("dp", "inner")),
            P(("dp", "inner")),
            P(("dp", "inner"), None),
            P(),
            P(),
        ),
        out_specs=(
            P(("dp", "inner"), None),
            P(("dp", "inner"), None),
            P(),
            P(("dp", "inner"), None),
            P(("dp", "inner")),
            P(("dp", "inner")),
            P(),
            P(),
        ),
        check_vma=False,
    )
```

profile of v0, /device:TPU:0, one launch (start us, length us, event | category | flops | bytes accessed | tf_op | source)
XLA Modules:
  0.0 36.5 jit_solution(4957636563195857111)
XLA Ops:
  0.6 1.1 %prep.1.refs_3_ = bf16[16,640]{1,0:T(8,128)(2,1)S(1)} custom-call(f32[16,512]{1,0:T(8,128)} %refs_4_.5, f32[1,16]{1,0:T(1,128)} %bitcast.7, f32[1,16]{1,0:T(1,128)} %bitcast.12, f32[16,256]{1,0:T(8,128)} %refs_6_.1), custom_call_target="tpu_custom_call" | custom-call | flops 4194304000 | bytes 8388608 | tf_op jit(solution)/shard_map/prep/pallas_call | solution.py:31
  1.7 4.1 %collective-permute-start = (bf16[16,640]{1,0:T(8,128)(2,1)S(1)}, bf16[16,640]{1,0:T(8,128)(2,1)S(1)}, u32[]{:S(2)}, u32[]{:S(2)}) collective-permute-start(bf16[16,640]{1,0:T(8,128)(2,1)S(1)} %prep.1.refs_3_), channel_id=1, source_target_pairs={{0,16},{1,17},{2,18},{3,19},{4,20},{5,21},{6,22},{7,23},{8,24},{9,... | collective-permute-start | bytes 61448 | tf_op jit(solution)/shard_map/ppermute | solution.py:361
  5.8 0.5 %collective-permute-start.1 = (bf16[16,640]{1,0:T(8,128)(2,1)S(1)}, bf16[16,640]{1,0:T(8,128)(2,1)S(1)}, u32[]{:S(2)}, u32[]{:S(2)}) collective-permute-start(bf16[16,640]{1,0:T(8,128)(2,1)S(1)} %prep.1.refs_3_), channel_id=1, source_target_pairs={{0,25},{1,24},{2,27},{3,26},{4,29},{5,28},{6,31},{7,30},{8,17},{9,... | collective-permute-start | bytes 61448 | tf_op jit(solution)/shard_map/ppermute | solution.py:361
  6.4 0.2 collective-permute-start.2
  6.6 1.9 %inputs.1 = (bf16[2048,384]{1,0:T(8,128)(2,1)S(1)}, bf16[272,2048]{1,0:T(8,128)(2,1)S(1)}) custom-call(f32[2048,253]{1,0:T(8,128)} %refs_0_.3, f32[3,2048]{1,0:T(4,128)} %bitcast.9, s32[1,2048]{1,0:T(1,128)} %bitcast.10, s32[1,2048]{1,0:T(1,128)} %bitcast.11), custom_call_target="tpu_custom_call" | custom-call | flops 4194304000 | bytes 4194304 | tf_op jit(solution)/shard_map/inputs/pallas_call | solution.py:416
  8.5 0.0 copy-start.1
  8.5 0.0 collective-permute-done.refs_0_
  8.5 2.3 %collective-permute-done.1.refs_1_ = bf16[16,640]{1,0:T(8,128)(2,1)S(1)} collective-permute-done((bf16[16,640]{1,0:T(8,128)(2,1)S(1)}, bf16[16,640]{1,0:T(8,128)(2,1)S(1)}, u32[]{:S(2)}, u32[]{:S(2)}) %collective-permute-start.1) | collective-permute-done | bytes 20512 | tf_op jit(solution)/shard_map/ppermute | solution.py:361
  10.9 0.0 collective-permute-done.2.refs_2_
  10.9 0.1 pack.1
  10.9 0.0 copy-start
  10.9 2.5 %collective-permute-start.3 = (bf16[144,128]{1,0:T(8,128)(2,1)S(1)}, bf16[144,128]{1,0:T(8,128)(2,1)S(1)}, u32[]{:S(2)}, u32[]{:S(2)}) collective-permute-start(bf16[144,128]{1,0:T(8,128)(2,1)S(1)} %get-tuple-element.55.refs_3_), channel_id=1, source_target_pairs={{0,6},{1,7},{2,4},{3,5},{4,2},{5,3},{6,0},{7,1},{8,14},{9,15},{10,... | collective-permute-start | bytes 110600 | tf_op jit(solution)/shard_map/ppermute | solution.py:361
  13.4 0.0 collective-permute-start.4
  13.4 0.8 %collective-permute-start.5 = (bf16[144,128]{1,0:T(8,128)(2,1)S(1)}, bf16[144,128]{1,0:T(8,128)(2,1)S(1)}, u32[]{:S(2)}, u32[]{:S(2)}) collective-permute-start(bf16[144,128]{1,0:T(8,128)(2,1)S(1)} %get-tuple-element.55.refs_3_), channel_id=1, source_target_pairs={{0,3},{1,2},{2,1},{3,0},{4,7},{5,6},{6,5},{7,4},{8,11},{9,10},{10,... | collective-permute-start | bytes 110600 | tf_op jit(solution)/shard_map/ppermute | solution.py:361
  14.2 1.6 %collective-permute-done.3.refs_0_ = bf16[144,128]{1,0:T(8,128)(2,1)S(1)} collective-permute-done((bf16[144,128]{1,0:T(8,128)(2,1)S(1)}, bf16[144,128]{1,0:T(8,128)(2,1)S(1)}, u32[]{:S(2)}, u32[]{:S(2)}) %collective-permute-start.3) | collective-permute-done | bytes 36896 | tf_op jit(solution)/shard_map/ppermute | solution.py:361
  15.8 1.4 %collective-permute-done.4.refs_1_ = bf16[144,128]{1,0:T(8,128)(2,1)S(1)} collective-permute-done((bf16[144,128]{1,0:T(8,128)(2,1)S(1)}, bf16[144,128]{1,0:T(8,128)(2,1)S(1)}, u32[]{:S(2)}, u32[]{:S(2)}) %collective-permute-start.4) | collective-permute-done | bytes 36896 | tf_op jit(solution)/shard_map/ppermute | solution.py:361
  17.2 0.0 collective-permute-done.5.refs_2_
  17.2 0.0 copy-done.1
  17.2 0.3 collective-permute-start.6
  17.5 0.0 copy-done
  17.6 1.2 %collective-permute-start.7 = (bf16[64,256]{1,0:T(8,128)(2,1)S(1)}, bf16[64,256]{1,0:T(8,128)(2,1)S(1)}, u32[]{:S(2)}, u32[]{:S(2)}) collective-permute-start(bf16[64,256]{1,0:T(8,128)(2,1)S(1)} %get-tuple-element.61.refs_1_), channel_id=1, source_target_pairs={{0,5},{1,4},{2,7},{3,6},{4,1},{5,0},{6,3},{7,2},{8,13},{9,12},{10,... | collective-permute-start | bytes 98312 | tf_op jit(solution)/shard_map/ppermute | solution.py:361
  18.7 0.0 collective-permute-done.6.refs_1_
  18.7 3.0 %layer.1 = (f32[2048,512]{1,0:T(8,128)}, f32[1024,512]{1,0:T(8,128)S(1)}, f32[2048,253]{1,0:T(8,128)S(1)}, bf16[288,256]{1,0:T(8,128)(2,1)S(1)}, bf16[288,256]{1,0:T(8,128)(2,1)S(1)}) custom-call(bf16[576,128]{1,0:T(8,128)(2,1)S(1)} %join.3.refs_0_, bf16[576,128]{1,0:T(8,128)(2,1)S(1)} %collective-permute-done.6.refs_1_, ...), custom_call_target="tpu_custom_call" | custom-call | flops 3221225472 | bytes 12582912 | tf_op jit(solution)/shard_map/layer/pallas_call | solution.py:487
  21.8 0.0 collective-permute-done.7.refs_0_
  21.8 0.0 copy-start.4
  21.8 0.0 copy-start.5
  21.8 0.6 %collective-permute-start.8 = (bf16[288,256]{1,0:T(8,128)(2,1)S(1)}, bf16[288,256]{1,0:T(8,128)(2,1)S(1)}, u32[]{:S(2)}, u32[]{:S(2)}) collective-permute-start(bf16[288,256]{1,0:T(8,128)(2,1)S(1)} %get-tuple-element.62), channel_id=1, source_target_pairs={{0,1},{1,0},{2,3},{3,2},{4,5},{5,4},{6,7},{7,6},{8,9},{9,8},{10,11... | collective-permute-start | bytes 442376 | tf_op jit(solution)/shard_map/ppermute | solution.py:361
  22.4 0.1 copy-done.4
  22.5 0.0 copy-done.5
  22.5 0.6 %multiply_add_fusion = (f32[256]{0:T(256)}, f32[256]{0:T(256)}) fusion(f32[256]{0:T(256)S(1)} %get-tuple-element.95, f32[256]{0:T(256)S(1)} %get-tuple-element.94, f32[256]{0:T(256)S(1)} %copy-done.4, f32[256]{0:T(256)S(1)} %copy-done.5), kind=kLoop, calls=%fused_computation.1 | loop fusion | flops 2560 | bytes 6144 | tf_op jit(solution)/shard_map/add | solution.py:594
  23.1 0.3 collective-permute-done.8.refs_0_
  23.4 1.3 %collective-permute-start.10 = (bf16[96,256]{1,0:T(8,128)(2,1)S(1)}, bf16[96,256]{1,0:T(8,128)(2,1)S(1)}, u32[]{:S(2)}, u32[]{:S(2)}) collective-permute-start(bf16[96,256]{1,0:T(8,128)(2,1)S(1)} %get-tuple-element.70), channel_id=1, source_target_pairs={{0,6},{1,7},{2,4},{3,5},{4,2},{5,3},{6,0},{7,1},{8,14},{9,15},{10,... | collective-permute-start | bytes 147464 | tf_op jit(solution)/shard_map/ppermute | solution.py:361
  24.8 0.4 %collective-permute-start.11 = (bf16[96,256]{1,0:T(8,128)(2,1)S(1)}, bf16[96,256]{1,0:T(8,128)(2,1)S(1)}, u32[]{:S(2)}, u32[]{:S(2)}) collective-permute-start(bf16[96,256]{1,0:T(8,128)(2,1)S(1)} %get-tuple-element.71), channel_id=1, source_target_pairs={{0,5},{1,4},{2,7},{3,6},{4,1},{5,0},{6,3},{7,2},{8,13},{9,12},{10,... | collective-permute-start | bytes 147464 | tf_op jit(solution)/shard_map/ppermute | solution.py:361
  25.2 1.6 %collective-permute-start.9 = (bf16[96,256]{1,0:T(8,128)(2,1)S(1)}, bf16[96,256]{1,0:T(8,128)(2,1)S(1)}, u32[]{:S(2)}, u32[]{:S(2)}) collective-permute-start(bf16[96,256]{1,0:T(8,128)(2,1)S(1)} %get-tuple-element.69), channel_id=1, source_target_pairs={{0,3},{1,2},{2,1},{3,0},{4,7},{5,6},{6,5},{7,4},{8,11},{9,10},{10,... | collective-permute-start | bytes 147464 | tf_op jit(solution)/shard_map/ppermute | solution.py:361
  26.7 1.3 %store.1 = f32[2048,253]{1,0:T(8,128)} custom-call(f32[2048,253]{1,0:T(8,128)S(1)} %get-tuple-element.77.source_ref), custom_call_target="tpu_custom_call" | custom-call | flops 4194304000 | bytes 4145152 | tf_op jit(solution)/shard_map/store/pallas_call | solution.py:515
  28.1 0.2 collective-permute-start.15
  28.3 0.2 collective-permute-done.10.refs_1_
  28.5 0.2 collective-permute-done.11.refs_2_
  28.7 0.5 %collective-permute-done.9.refs_0_ = bf16[96,256]{1,0:T(8,128)(2,1)S(1)} collective-permute-done((bf16[96,256]{1,0:T(8,128)(2,1)S(1)}, bf16[96,256]{1,0:T(8,128)(2,1)S(1)}, u32[]{:S(2)}, u32[]{:S(2)}) %collective-permute-start.9) | collective-permute-done | bytes 49184 | tf_op jit(solution)/shard_map/ppermute | solution.py:361
  29.2 1.0 %collective-permute-start.12 = (bf16[48,256]{1,0:T(8,128)(2,1)S(1)}, bf16[48,256]{1,0:T(8,128)(2,1)S(1)}, u32[]{:S(2)}, u32[]{:S(2)}) collective-permute-start(bf16[48,256]{1,0:T(8,128)(2,1)S(1)} %get-tuple-element.83), channel_id=1, source_target_pairs={{0,16},{1,17},{2,18},{3,19},{4,20},{5,21},{6,22},{7,23},{8,24},{9,... | collective-permute-start | bytes 73736 | tf_op jit(solution)/shard_map/ppermute | solution.py:361
  30.2 1.0 %collective-permute-start.13 = (bf16[48,256]{1,0:T(8,128)(2,1)S(1)}, bf16[48,256]{1,0:T(8,128)(2,1)S(1)}, u32[]{:S(2)}, u32[]{:S(2)}) collective-permute-start(bf16[48,256]{1,0:T(8,128)(2,1)S(1)} %get-tuple-element.84), channel_id=1, source_target_pairs={{0,25},{1,24},{2,27},{3,26},{4,29},{5,28},{6,31},{7,30},{8,17},{9,... | collective-permute-start | bytes 73736 | tf_op jit(solution)/shard_map/ppermute | solution.py:361
  31.2 1.3 %collective-permute-start.14 = (bf16[48,256]{1,0:T(8,128)(2,1)S(1)}, bf16[48,256]{1,0:T(8,128)(2,1)S(1)}, u32[]{:S(2)}, u32[]{:S(2)}) collective-permute-start(bf16[48,256]{1,0:T(8,128)(2,1)S(1)} %get-tuple-element.85), channel_id=1, source_target_pairs={{0,9},{1,8},{2,11},{3,10},{4,13},{5,12},{6,15},{7,14},{8,1},{9,0},... | collective-permute-start | bytes 73736 | tf_op jit(solution)/shard_map/ppermute | solution.py:361
  32.5 0.0 collective-permute-done.15.refs_0_
  32.5 0.1 collective-permute-start.16
  32.6 0.0 copy-start.2
  32.6 0.0 copy-start.3
  32.6 1.3 %tail.1 = f32[2048,512]{1,0:T(8,128)} custom-call(f32[2048,512]{1,0:T(8,128)} %get-tuple-element.58._, f32[1024,512]{1,0:T(8,128)S(1)} %get-tuple-element.81.source_ref), custom_call_target="tpu_custom_call", output_to_operand_aliasing={{}: (0, {})} | custom-call | flops 4194304000 | bytes 4145152 | tf_op jit(solution)/shard_map/tail/pallas_call | solution.py:515
  33.9 0.1 collective-permute-done.12.refs_0_
  34.0 1.4 %collective-permute-done.13.refs_1_ = bf16[48,256]{1,0:T(8,128)(2,1)S(1)} collective-permute-done((bf16[48,256]{1,0:T(8,128)(2,1)S(1)}, bf16[48,256]{1,0:T(8,128)(2,1)S(1)}, u32[]{:S(2)}, u32[]{:S(2)}) %collective-permute-start.13) | collective-permute-done | bytes 24608 | tf_op jit(solution)/shard_map/ppermute | solution.py:361
  35.4 0.0 collective-permute-done.14.refs_2_
  35.4 0.0 collective-permute-done.16.refs_8_
  35.4 0.0 copy-done.2
  35.4 0.0 copy-done.3
  35.4 1.1 %last.1 = (f32[16,256]{1,0:T(8,128)}, f32[16,512]{1,0:T(8,128)}, f32[1,16]{1,0:T(1,128)}, f32[1,16]{1,0:T(1,128)}) custom-call(bf16[48,256]{1,0:T(8,128)(2,1)S(1)} %collective-permute-done.12.refs_0_, bf16[48,256]{1,0:T(8,128)(2,1)S(1)} %collective-permute-done.13.refs_1_, bf16[48,256]{1,0:T(8,128)(2,1)S(1)} %collective-permute-done.14.refs_2_, ...), custom_call_target="tpu_custom_call" | custom-call | flops 4194304000 | bytes 8388608 | tf_op jit(solution)/shard_map/last/pallas_call | solution.py:31
  (6 shorter events, 0.1 us)
Async XLA Ops:
  1.7 6.8 %collective-permute-start = (bf16[16,640]{1,0:T(8,128)(2,1)S(1)}, bf16[16,640]{1,0:T(8,128)(2,1)S(1)}, u32[]{:S(2)}, u32[]{:S(2)}) collective-permute-start(bf16[16,640]{1,0:T(8,128)(2,1)S(1)} %prep.1.refs_3_), channel_id=1, source_target_pairs={{0,16},{1,17},{2,18},{3,19},{4,20},{5,21},{6,22},{7,23},{8,24},{9,... | collective-permute-start | bytes 61448 | tf_op jit(solution)/shard_map/ppermute | solution.py:361
  5.8 5.0 %collective-permute-start.1 = (bf16[16,640]{1,0:T(8,128)(2,1)S(1)}, bf16[16,640]{1,0:T(8,128)(2,1)S(1)}, u32[]{:S(2)}, u32[]{:S(2)}) collective-permute-start(bf16[16,640]{1,0:T(8,128)(2,1)S(1)} %prep.1.refs_3_), channel_id=1, source_target_pairs={{0,25},{1,24},{2,27},{3,26},{4,29},{5,28},{6,31},{7,30},{8,17},{9,... | collective-permute-start | bytes 61448 | tf_op jit(solution)/shard_map/ppermute | solution.py:361
  6.4 4.5 %collective-permute-start.2 = (bf16[16,640]{1,0:T(8,128)(2,1)S(1)}, bf16[16,640]{1,0:T(8,128)(2,1)S(1)}, u32[]{:S(2)}, u32[]{:S(2)}) collective-permute-start(bf16[16,640]{1,0:T(8,128)(2,1)S(1)} %prep.1.refs_3_), channel_id=1, source_target_pairs={{0,9},{1,8},{2,11},{3,10},{4,13},{5,12},{6,15},{7,14},{8,1},{9,0},... | collective-permute-start | bytes 61448 | tf_op jit(solution)/shard_map/ppermute | solution.py:361
  8.5 8.7 %copy-start.1 = (f32[2048,512]{1,0:T(8,128)S(1)}, f32[2048,512]{1,0:T(8,128)}, u32[]{:S(2)}) copy-start(f32[2048,512]{1,0:T(8,128)} %refs_4_.4) | copy-start | bytes 12582916
  10.9 6.6 %copy-start = (f32[16,256]{1,0:T(8,128)S(1)}, f32[16,256]{1,0:T(8,128)}, u32[]{:S(2)}) copy-start(f32[16,256]{1,0:T(8,128)} %refs_6_.1) | copy-start | bytes 49156
  10.9 4.9 %collective-permute-start.3 = (bf16[144,128]{1,0:T(8,128)(2,1)S(1)}, bf16[144,128]{1,0:T(8,128)(2,1)S(1)}, u32[]{:S(2)}, u32[]{:S(2)}) collective-permute-start(bf16[144,128]{1,0:T(8,128)(2,1)S(1)} %get-tuple-element.55.refs_3_), channel_id=1, source_target_pairs={{0,6},{1,7},{2,4},{3,5},{4,2},{5,3},{6,0},{7,1},{8,14},{9,15},{10,... | collective-permute-start | bytes 110600 | tf_op jit(solution)/shard_map/ppermute | solution.py:361
  13.4 3.8 %collective-permute-start.4 = (bf16[144,128]{1,0:T(8,128)(2,1)S(1)}, bf16[144,128]{1,0:T(8,128)(2,1)S(1)}, u32[]{:S(2)}, u32[]{:S(2)}) collective-permute-start(bf16[144,128]{1,0:T(8,128)(2,1)S(1)} %get-tuple-element.55.refs_3_), channel_id=1, source_target_pairs={{0,5},{1,4},{2,7},{3,6},{4,1},{5,0},{6,3},{7,2},{8,13},{9,12},{10,... | collective-permute-start | bytes 110600 | tf_op jit(solution)/shard_map/ppermute | solution.py:361
  13.4 3.8 %collective-permute-start.5 = (bf16[144,128]{1,0:T(8,128)(2,1)S(1)}, bf16[144,128]{1,0:T(8,128)(2,1)S(1)}, u32[]{:S(2)}, u32[]{:S(2)}) collective-permute-start(bf16[144,128]{1,0:T(8,128)(2,1)S(1)} %get-tuple-element.55.refs_3_), channel_id=1, source_target_pairs={{0,3},{1,2},{2,1},{3,0},{4,7},{5,6},{6,5},{7,4},{8,11},{9,10},{10,... | collective-permute-start | bytes 110600 | tf_op jit(solution)/shard_map/ppermute | solution.py:361
  17.2 1.5 %collective-permute-start.6 = (bf16[576,128]{1,0:T(8,128)(2,1)S(1)}, bf16[576,128]{1,0:T(8,128)(2,1)S(1)}, u32[]{:S(2)}, u32[]{:S(2)}) collective-permute-start(bf16[576,128]{1,0:T(8,128)(2,1)S(1)} %join.3.refs_0_), channel_id=1, source_target_pairs={{0,1},{1,0},{2,3},{3,2},{4,5},{5,4},{6,7},{7,6},{8,9},{9,8},{10,11... | collective-permute-start | bytes 442376 | tf_op jit(solution)/shard_map/ppermute | solution.py:361
  17.6 4.2 %collective-permute-start.7 = (bf16[64,256]{1,0:T(8,128)(2,1)S(1)}, bf16[64,256]{1,0:T(8,128)(2,1)S(1)}, u32[]{:S(2)}, u32[]{:S(2)}) collective-permute-start(bf16[64,256]{1,0:T(8,128)(2,1)S(1)} %get-tuple-element.61.refs_1_), channel_id=1, source_target_pairs={{0,5},{1,4},{2,7},{3,6},{4,1},{5,0},{6,3},{7,2},{8,13},{9,12},{10,... | collective-permute-start | bytes 98312 | tf_op jit(solution)/shard_map/ppermute | solution.py:361
  21.8 0.7 %copy-start.4 = (f32[256]{0:T(256)S(1)}, f32[256]{0:T(256)}, u32[]{:S(2)}) copy-start(f32[256]{0:T(256)} %param.21) | copy-start | bytes 3076
  21.8 0.7 %copy-start.5 = (f32[256]{0:T(256)S(1)}, f32[256]{0:T(256)}, u32[]{:S(2)}) copy-start(f32[256]{0:T(256)} %param.20) | copy-start | bytes 3076
  21.8 1.6 %collective-permute-start.8 = (bf16[288,256]{1,0:T(8,128)(2,1)S(1)}, bf16[288,256]{1,0:T(8,128)(2,1)S(1)}, u32[]{:S(2)}, u32[]{:S(2)}) collective-permute-start(bf16[288,256]{1,0:T(8,128)(2,1)S(1)} %get-tuple-element.62), channel_id=1, source_target_pairs={{0,1},{1,0},{2,3},{3,2},{4,5},{5,4},{6,7},{7,6},{8,9},{9,8},{10,11... | collective-permute-start | bytes 442376 | tf_op jit(solution)/shard_map/ppermute | solution.py:361
  23.4 5.1 %collective-permute-start.10 = (bf16[96,256]{1,0:T(8,128)(2,1)S(1)}, bf16[96,256]{1,0:T(8,128)(2,1)S(1)}, u32[]{:S(2)}, u32[]{:S(2)}) collective-permute-start(bf16[96,256]{1,0:T(8,128)(2,1)S(1)} %get-tuple-element.70), channel_id=1, source_target_pairs={{0,6},{1,7},{2,4},{3,5},{4,2},{5,3},{6,0},{7,1},{8,14},{9,15},{10,... | collective-permute-start | bytes 147464 | tf_op jit(solution)/shard_map/ppermute | solution.py:361
  24.8 3.9 %collective-permute-start.11 = (bf16[96,256]{1,0:T(8,128)(2,1)S(1)}, bf16[96,256]{1,0:T(8,128)(2,1)S(1)}, u32[]{:S(2)}, u32[]{:S(2)}) collective-permute-start(bf16[96,256]{1,0:T(8,128)(2,1)S(1)} %get-tuple-element.71), channel_id=1, source_target_pairs={{0,5},{1,4},{2,7},{3,6},{4,1},{5,0},{6,3},{7,2},{8,13},{9,12},{10,... | collective-permute-start | bytes 147464 | tf_op jit(solution)/shard_map/ppermute | solution.py:361
  25.2 4.0 %collective-permute-start.9 = (bf16[96,256]{1,0:T(8,128)(2,1)S(1)}, bf16[96,256]{1,0:T(8,128)(2,1)S(1)}, u32[]{:S(2)}, u32[]{:S(2)}) collective-permute-start(bf16[96,256]{1,0:T(8,128)(2,1)S(1)} %get-tuple-element.69), channel_id=1, source_target_pairs={{0,3},{1,2},{2,1},{3,0},{4,7},{5,6},{6,5},{7,4},{8,11},{9,10},{10,... | collective-permute-start | bytes 147464 | tf_op jit(solution)/shard_map/ppermute | solution.py:361
  28.1 4.4 %collective-permute-start.15 = (bf16[128,256]{1,0:T(8,128)(2,1)S(1)}, bf16[128,256]{1,0:T(8,128)(2,1)S(1)}, u32[]{:S(2)}, u32[]{:S(2)}) collective-permute-start(bf16[128,256]{1,0:T(8,128)(2,1)S(1)} %join.4.refs_1_), channel_id=1, source_target_pairs={{0,3},{1,2},{2,1},{3,0},{4,7},{5,6},{6,5},{7,4},{8,11},{9,10},{10,... | collective-permute-start | bytes 196616 | tf_op jit(solution)/shard_map/ppermute | solution.py:361
  29.2 4.8 %collective-permute-start.12 = (bf16[48,256]{1,0:T(8,128)(2,1)S(1)}, bf16[48,256]{1,0:T(8,128)(2,1)S(1)}, u32[]{:S(2)}, u32[]{:S(2)}) collective-permute-start(bf16[48,256]{1,0:T(8,128)(2,1)S(1)} %get-tuple-element.83), channel_id=1, source_target_pairs={{0,16},{1,17},{2,18},{3,19},{4,20},{5,21},{6,22},{7,23},{8,24},{9,... | collective-permute-start | bytes 73736 | tf_op jit(solution)/shard_map/ppermute | solution.py:361
  30.2 5.2 %collective-permute-start.13 = (bf16[48,256]{1,0:T(8,128)(2,1)S(1)}, bf16[48,256]{1,0:T(8,128)(2,1)S(1)}, u32[]{:S(2)}, u32[]{:S(2)}) collective-permute-start(bf16[48,256]{1,0:T(8,128)(2,1)S(1)} %get-tuple-element.84), channel_id=1, source_target_pairs={{0,25},{1,24},{2,27},{3,26},{4,29},{5,28},{6,31},{7,30},{8,17},{9,... | collective-permute-start | bytes 73736 | tf_op jit(solution)/shard_map/ppermute | solution.py:361
  31.2 4.2 %collective-permute-start.14 = (bf16[48,256]{1,0:T(8,128)(2,1)S(1)}, bf16[48,256]{1,0:T(8,128)(2,1)S(1)}, u32[]{:S(2)}, u32[]{:S(2)}) collective-permute-start(bf16[48,256]{1,0:T(8,128)(2,1)S(1)} %get-tuple-element.85), channel_id=1, source_target_pairs={{0,9},{1,8},{2,11},{3,10},{4,13},{5,12},{6,15},{7,14},{8,1},{9,0},... | collective-permute-start | bytes 73736 | tf_op jit(solution)/shard_map/ppermute | solution.py:361
  32.5 2.9 %collective-permute-start.16 = (bf16[256,256]{1,0:T(8,128)(2,1)S(1)}, bf16[256,256]{1,0:T(8,128)(2,1)S(1)}, u32[]{:S(2)}, u32[]{:S(2)}) collective-permute-start(bf16[256,256]{1,0:T(8,128)(2,1)S(1)} %join.5.refs_7_), channel_id=1, source_target_pairs={{0,1},{1,0},{2,3},{3,2},{4,5},{5,4},{6,7},{7,6},{8,9},{9,8},{10,11... | collective-permute-start | bytes 393224 | tf_op jit(solution)/shard_map/ppermute | solution.py:361
  32.6 2.8 %copy-start.2 = (f32[16,512]{1,0:T(8,128)S(1)}, f32[16,512]{1,0:T(8,128)}, u32[]{:S(2)}) copy-start(f32[16,512]{1,0:T(8,128)} %refs_4_.5) | copy-start | bytes 98308
  32.6 2.8 %copy-start.3 = (f32[16]{0:T(128)S(1)}, f32[16]{0:T(128)}, u32[]{:S(2)}) copy-start(f32[16]{0:T(128)} %param.17) | copy-start | bytes 196
where the time goes:
time: 36.8 us; the launch traced here: 36.5 us
  starting transfers between devices  17 us (46%)
  Pallas kernels  9.96 us (27%)
  waiting for transfers between devices  8.04 us (22%)
  between operations  0.79 us (2%)
  other arithmetic  0.59 us (2%)
    ppermute x17, starting transfers between devices, swaps(): lax.ppermute(x, AXES, [(i, i ^ mask) for i in range(devices)])  17 us
    ppermute x17, waiting for transfers between devices, swaps(): lax.ppermute(x, AXES, [(i, i ^ mask) for i in range(devices)])  8.04 us
    pallas_call x1, Pallas kernels, per_device(): pl.pallas_call(functools.partial(layer_kernel, hid, shapes, layer_tile, o...  3.04 us
    pallas_call x2, Pallas kernels, store(): pl.pallas_call(body, out_shape=pltpu.HBM(shape, F32), in_specs=[pl.BlockS...  2.66 us
    pallas_call x8, Pallas kernels, small_kernel(): pl.pallas_call(body, out_shape=out_shape, in_specs=[pl.BlockSpec(memory_s...  2.35 us
    pallas_call x1, Pallas kernels, per_device(): pl.pallas_call(functools.partial(inputs_kernel, hid, tile), out_shape=[sh...  1.91 us
  transfers between devices with their start and end apart: 17, of which 9 were waited for; matrix products, arithmetic and copies ran while one was open for 2% of the time, Pallas kernels for 21%

commit v1 on v0

--- a/solution.py
+++ b/solution.py
@@ -469,10 +469,10 @@
             ],
             *[arrays[k] for k in FIRST],
         )
-        weight, code_weight, x, x_t = lax.optimization_barrier((weight, code_weight, x, x_t))
         (weights,) = [gather(weight, group) for group in groups[1:-1]]
         along, across = [[bit] for bit in groups[1][::-1]]
         (weight,) = join(weights, LANES, early=(cotangent,))
+        weight, x, x_t = lax.optimization_barrier((weight, x, x_t))
         weights = gather(weight, groups[-1])
         code_weights = gather(code_weight, along)
         code_order = order_of([groups[0], along, across])

time: 36.8 us -> 36.9 us (level)
  waiting for transfers between devices: 8.04 us -> 6.95 us
  starting transfers between devices: 17 us -> 17.9 us
    ppermute x17, waiting for transfers between devices: 8.04 us -> 6.95 us  [swaps(): lax.ppermute(x, AXES, [(i, i ^ mask) for i in range(devices)])]
    ppermute x17, starting transfers between devices: 17 us -> 17.9 us  [swaps(): lax.ppermute(x, AXES, [(i, i ^ mask) for i in range(devices)])]
  transfers between devices with their start and end apart: 17 -> 17, of which waited for: 9 -> 7; matrix products, arithmetic and copies ran while one was open for 2% -> 2% of each run, Pallas kernels for 21% -> 21%
where the time goes in v1:
time: 36.9 us; the launch traced here: 36.6 us
  starting transfers between devices  17.9 us (49%)
  Pallas kernels  10.1 us (27%)
  waiting for transfers between devices  6.95 us (19%)
  between operations  0.76 us (2%)
  other arithmetic  0.59 us (2%)
    ppermute x17, starting transfers between devices, swaps(): lax.ppermute(x, AXES, [(i, i ^ mask) for i in range(devices)])  17.9 us
    ppermute x17, waiting for transfers between devices, swaps(): lax.ppermute(x, AXES, [(i, i ^ mask) for i in range(devices)])  6.95 us
    pallas_call x1, Pallas kernels, per_device(): pl.pallas_call(functools.partial(layer_kernel, hid, shapes, layer_tile, o...  3.05 us
    pallas_call x2, Pallas kernels, store(): pl.pallas_call(body, out_shape=pltpu.HBM(shape, F32), in_specs=[pl.BlockS...  2.65 us
    pallas_call x8, Pallas kernels, small_kernel(): pl.pallas_call(body, out_shape=out_shape, in_specs=[pl.BlockSpec(memory_s...  2.35 us
    pallas_call x1, Pallas kernels, per_device(): pl.pallas_call(functools.partial(inputs_kernel, hid, tile), out_shape=[sh...  2.06 us
  transfers between devices with their start and end apart: 17, of which 7 were waited for; matrix products, arithmetic and copies ran while one was open for 2% of the time, Pallas kernels for 21%

profile of v1, /device:TPU:0, one launch (start us, length us, event | category | flops | bytes accessed | tf_op | source)
XLA Modules:
  0.0 36.6 jit_solution(7653554487718806634)
XLA Ops:
  0.6 1.1 %prep.1.refs_3_ = bf16[16,640]{1,0:T(8,128)(2,1)S(1)} custom-call(f32[16,512]{1,0:T(8,128)} %refs_4_.5, f32[1,16]{1,0:T(1,128)} %bitcast.7, f32[1,16]{1,0:T(1,128)} %bitcast.12, f32[16,256]{1,0:T(8,128)} %refs_6_.1), custom_call_target="tpu_custom_call" | custom-call | flops 4194304000 | bytes 8388608 | tf_op jit(solution)/shard_map/prep/pallas_call | solution.py:31
  1.7 4.1 %collective-permute-start = (bf16[16,640]{1,0:T(8,128)(2,1)S(1)}, bf16[16,640]{1,0:T(8,128)(2,1)S(1)}, u32[]{:S(2)}, u32[]{:S(2)}) collective-permute-start(bf16[16,640]{1,0:T(8,128)(2,1)S(1)} %prep.1.refs_3_), channel_id=1, source_target_pairs={{0,16},{1,17},{2,18},{3,19},{4,20},{5,21},{6,22},{7,23},{8,24},{9,... | collective-permute-start | bytes 61448 | tf_op jit(solution)/shard_map/ppermute | solution.py:361
  5.8 0.5 %collective-permute-start.1 = (bf16[16,640]{1,0:T(8,128)(2,1)S(1)}, bf16[16,640]{1,0:T(8,128)(2,1)S(1)}, u32[]{:S(2)}, u32[]{:S(2)}) collective-permute-start(bf16[16,640]{1,0:T(8,128)(2,1)S(1)} %prep.1.refs_3_), channel_id=1, source_target_pairs={{0,25},{1,24},{2,27},{3,26},{4,29},{5,28},{6,31},{7,30},{8,17},{9,... | collective-permute-start | bytes 61448 | tf_op jit(solution)/shard_map/ppermute | solution.py:361
  6.4 0.2 collective-permute-start.2
  6.6 1.0 %collective-permute-done.refs_0_ = bf16[16,640]{1,0:T(8,128)(2,1)S(1)} collective-permute-done((bf16[16,640]{1,0:T(8,128)(2,1)S(1)}, bf16[16,640]{1,0:T(8,128)(2,1)S(1)}, u32[]{:S(2)}, u32[]{:S(2)}) %collective-permute-start) | collective-permute-done | bytes 20512 | tf_op jit(solution)/shard_map/ppermute | solution.py:361
  7.6 3.3 %collective-permute-done.1.refs_1_ = bf16[16,640]{1,0:T(8,128)(2,1)S(1)} collective-permute-done((bf16[16,640]{1,0:T(8,128)(2,1)S(1)}, bf16[16,640]{1,0:T(8,128)(2,1)S(1)}, u32[]{:S(2)}, u32[]{:S(2)}) %collective-permute-start.1) | collective-permute-done | bytes 20512 | tf_op jit(solution)/shard_map/ppermute | solution.py:361
  10.9 0.0 collective-permute-done.2.refs_2_
  10.9 0.1 pack.1
  10.9 2.5 %collective-permute-start.3 = (bf16[144,128]{1,0:T(8,128)(2,1)S(1)}, bf16[144,128]{1,0:T(8,128)(2,1)S(1)}, u32[]{:S(2)}, u32[]{:S(2)}) collective-permute-start(bf16[144,128]{1,0:T(8,128)(2,1)S(1)} %get-tuple-element.50.refs_3_), channel_id=1, source_target_pairs={{0,6},{1,7},{2,4},{3,5},{4,2},{5,3},{6,0},{7,1},{8,14},{9,15},{10,... | collective-permute-start | bytes 110600 | tf_op jit(solution)/shard_map/ppermute | solution.py:361
  13.4 0.0 collective-permute-start.4
  13.4 0.8 %collective-permute-start.5 = (bf16[144,128]{1,0:T(8,128)(2,1)S(1)}, bf16[144,128]{1,0:T(8,128)(2,1)S(1)}, u32[]{:S(2)}, u32[]{:S(2)}) collective-permute-start(bf16[144,128]{1,0:T(8,128)(2,1)S(1)} %get-tuple-element.50.refs_3_), channel_id=1, source_target_pairs={{0,3},{1,2},{2,1},{3,0},{4,7},{5,6},{6,5},{7,4},{8,11},{9,10},{10,... | collective-permute-start | bytes 110600 | tf_op jit(solution)/shard_map/ppermute | solution.py:361
  14.2 0.0 copy-start.1
  14.2 2.1 %inputs.1 = (bf16[2048,384]{1,0:T(8,128)(2,1)S(1)}, bf16[272,2048]{1,0:T(8,128)(2,1)S(1)}) custom-call(f32[2048,253]{1,0:T(8,128)} %refs_0_.3, f32[3,2048]{1,0:T(4,128)} %bitcast.9, s32[1,2048]{1,0:T(1,128)} %bitcast.10, s32[1,2048]{1,0:T(1,128)} %bitcast.11), custom_call_target="tpu_custom_call" | custom-call | flops 4194304000 | bytes 4194304 | tf_op jit(solution)/shard_map/inputs/pallas_call | solution.py:416
  16.2 0.0 copy-start
  16.2 0.0 collective-permute-done.3.refs_0_
  16.3 0.9 %collective-permute-done.4.refs_1_ = bf16[144,128]{1,0:T(8,128)(2,1)S(1)} collective-permute-done((bf16[144,128]{1,0:T(8,128)(2,1)S(1)}, bf16[144,128]{1,0:T(8,128)(2,1)S(1)}, u32[]{:S(2)}, u32[]{:S(2)}) %collective-permute-start.4) | collective-permute-done | bytes 36896 | tf_op jit(solution)/shard_map/ppermute | solution.py:361
  17.2 0.0 collective-permute-done.5.refs_2_
  17.2 0.0 copy-done.1
  17.2 0.3 collective-permute-start.6
  17.5 0.0 copy-done
  17.5 1.3 %collective-permute-start.7 = (bf16[64,256]{1,0:T(8,128)(2,1)S(1)}, bf16[64,256]{1,0:T(8,128)(2,1)S(1)}, u32[]{:S(2)}, u32[]{:S(2)}) collective-permute-start(bf16[64,256]{1,0:T(8,128)(2,1)S(1)} %get-tuple-element.59.refs_1_), channel_id=1, source_target_pairs={{0,5},{1,4},{2,7},{3,6},{4,1},{5,0},{6,3},{7,2},{8,13},{9,12},{10,... | collective-permute-start | bytes 98312 | tf_op jit(solution)/shard_map/ppermute | solution.py:361
  18.8 0.0 collective-permute-done.6.refs_1_
  18.8 3.0 %layer.1 = (f32[2048,512]{1,0:T(8,128)}, f32[1024,512]{1,0:T(8,128)S(1)}, f32[2048,253]{1,0:T(8,128)S(1)}, bf16[288,256]{1,0:T(8,128)(2,1)S(1)}, bf16[288,256]{1,0:T(8,128)(2,1)S(1)}) custom-call(bf16[576,128]{1,0:T(8,128)(2,1)S(1)} %join.3.refs_0_, bf16[576,128]{1,0:T(8,128)(2,1)S(1)} %collective-permute-done.6.refs_1_, ...), custom_call_target="tpu_custom_call" | custom-call | flops 3221225472 | bytes 12582912 | tf_op jit(solution)/shard_map/layer/pallas_call | solution.py:487
  21.9 0.0 collective-permute-done.7.refs_0_
  21.9 0.0 copy-start.4
  21.9 0.0 copy-start.5
  21.9 0.5 %collective-permute-start.8 = (bf16[288,256]{1,0:T(8,128)(2,1)S(1)}, bf16[288,256]{1,0:T(8,128)(2,1)S(1)}, u32[]{:S(2)}, u32[]{:S(2)}) collective-permute-start(bf16[288,256]{1,0:T(8,128)(2,1)S(1)} %get-tuple-element.60), channel_id=1, source_target_pairs={{0,1},{1,0},{2,3},{3,2},{4,5},{5,4},{6,7},{7,6},{8,9},{9,8},{10,11... | collective-permute-start | bytes 442376 | tf_op jit(solution)/shard_map/ppermute | solution.py:361
  22.4 0.2 copy-done.4
  22.5 0.0 copy-done.5
  22.6 0.6 %multiply_add_fusion = (f32[256]{0:T(256)}, f32[256]{0:T(256)}) fusion(f32[256]{0:T(256)S(1)} %get-tuple-element.93, f32[256]{0:T(256)S(1)} %get-tuple-element.92, f32[256]{0:T(256)S(1)} %copy-done.4, f32[256]{0:T(256)S(1)} %copy-done.5), kind=kLoop, calls=%fused_computation.1 | loop fusion | flops 2560 | bytes 6144 | tf_op jit(solution)/shard_map/add | solution.py:594
  23.1 0.2 collective-permute-done.8.refs_0_
  23.4 2.1 %collective-permute-start.10 = (bf16[96,256]{1,0:T(8,128)(2,1)S(1)}, bf16[96,256]{1,0:T(8,128)(2,1)S(1)}, u32[]{:S(2)}, u32[]{:S(2)}) collective-permute-start(bf16[96,256]{1,0:T(8,128)(2,1)S(1)} %get-tuple-element.68), channel_id=1, source_target_pairs={{0,6},{1,7},{2,4},{3,5},{4,2},{5,3},{6,0},{7,1},{8,14},{9,15},{10,... | collective-permute-start | bytes 147464 | tf_op jit(solution)/shard_map/ppermute | solution.py:361
  25.6 0.3 collective-permute-start.11
  25.9 0.8 %collective-permute-start.9 = (bf16[96,256]{1,0:T(8,128)(2,1)S(1)}, bf16[96,256]{1,0:T(8,128)(2,1)S(1)}, u32[]{:S(2)}, u32[]{:S(2)}) collective-permute-start(bf16[96,256]{1,0:T(8,128)(2,1)S(1)} %get-tuple-element.67), channel_id=1, source_target_pairs={{0,3},{1,2},{2,1},{3,0},{4,7},{5,6},{6,5},{7,4},{8,11},{9,10},{10,... | collective-permute-start | bytes 147464 | tf_op jit(solution)/shard_map/ppermute | solution.py:361
  26.7 1.3 %store.1 = f32[2048,253]{1,0:T(8,128)} custom-call(f32[2048,253]{1,0:T(8,128)S(1)} %get-tuple-element.75.source_ref), custom_call_target="tpu_custom_call" | custom-call | flops 4194304000 | bytes 4145152 | tf_op jit(solution)/shard_map/store/pallas_call | solution.py:515
  28.0 1.0 %collective-permute-start.15 = (bf16[128,256]{1,0:T(8,128)(2,1)S(1)}, bf16[128,256]{1,0:T(8,128)(2,1)S(1)}, u32[]{:S(2)}, u32[]{:S(2)}) collective-permute-start(bf16[128,256]{1,0:T(8,128)(2,1)S(1)} %join.4.refs_1_), channel_id=1, source_target_pairs={{0,3},{1,2},{2,1},{3,0},{4,7},{5,6},{6,5},{7,4},{8,11},{9,10},{10,... | collective-permute-start | bytes 196616 | tf_op jit(solution)/shard_map/ppermute | solution.py:361
  29.0 0.0 collective-permute-done.10.refs_1_
  29.0 0.5 %collective-permute-done.11.refs_2_ = bf16[96,256]{1,0:T(8,128)(2,1)S(1)} collective-permute-done((bf16[96,256]{1,0:T(8,128)(2,1)S(1)}, bf16[96,256]{1,0:T(8,128)(2,1)S(1)}, u32[]{:S(2)}, u32[]{:S(2)}) %collective-permute-start.11) | collective-permute-done | bytes 49184 | tf_op jit(solution)/shard_map/ppermute | solution.py:361
  29.5 0.0 collective-permute-done.9.refs_0_
  29.6 0.8 %collective-permute-start.12 = (bf16[48,256]{1,0:T(8,128)(2,1)S(1)}, bf16[48,256]{1,0:T(8,128)(2,1)S(1)}, u32[]{:S(2)}, u32[]{:S(2)}) collective-permute-start(bf16[48,256]{1,0:T(8,128)(2,1)S(1)} %get-tuple-element.81), channel_id=1, source_target_pairs={{0,16},{1,17},{2,18},{3,19},{4,20},{5,21},{6,22},{7,23},{8,24},{9,... | collective-permute-start | bytes 73736 | tf_op jit(solution)/shard_map/ppermute | solution.py:361
  30.4 1.4 %collective-permute-start.13 = (bf16[48,256]{1,0:T(8,128)(2,1)S(1)}, bf16[48,256]{1,0:T(8,128)(2,1)S(1)}, u32[]{:S(2)}, u32[]{:S(2)}) collective-permute-start(bf16[48,256]{1,0:T(8,128)(2,1)S(1)} %get-tuple-element.82), channel_id=1, source_target_pairs={{0,25},{1,24},{2,27},{3,26},{4,29},{5,28},{6,31},{7,30},{8,17},{9,... | collective-permute-start | bytes 73736 | tf_op jit(solution)/shard_map/ppermute | solution.py:361
  31.8 1.1 %collective-permute-start.14 = (bf16[48,256]{1,0:T(8,128)(2,1)S(1)}, bf16[48,256]{1,0:T(8,128)(2,1)S(1)}, u32[]{:S(2)}, u32[]{:S(2)}) collective-permute-start(bf16[48,256]{1,0:T(8,128)(2,1)S(1)} %get-tuple-element.83), channel_id=1, source_target_pairs={{0,9},{1,8},{2,11},{3,10},{4,13},{5,12},{6,15},{7,14},{8,1},{9,0},... | collective-permute-start | bytes 73736 | tf_op jit(solution)/shard_map/ppermute | solution.py:361
  32.9 0.0 collective-permute-done.15.refs_0_
  32.9 0.3 collective-permute-start.16
  33.1 0.0 copy-start.2
  33.1 0.0 copy-start.3
  33.2 1.3 %tail.1 = f32[2048,512]{1,0:T(8,128)} custom-call(f32[2048,512]{1,0:T(8,128)} %get-tuple-element.56._, f32[1024,512]{1,0:T(8,128)S(1)} %get-tuple-element.79.source_ref), custom_call_target="tpu_custom_call", output_to_operand_aliasing={{}: (0, {})} | custom-call | flops 4194304000 | bytes 4145152 | tf_op jit(solution)/shard_map/tail/pallas_call | solution.py:515
  34.5 0.1 collective-permute-done.12.refs_0_
  34.6 0.9 %collective-permute-done.13.refs_1_ = bf16[48,256]{1,0:T(8,128)(2,1)S(1)} collective-permute-done((bf16[48,256]{1,0:T(8,128)(2,1)S(1)}, bf16[48,256]{1,0:T(8,128)(2,1)S(1)}, u32[]{:S(2)}, u32[]{:S(2)}) %collective-permute-start.13) | collective-permute-done | bytes 24608 | tf_op jit(solution)/shard_map/ppermute | solution.py:361
  35.5 0.0 collective-permute-done.14.refs_2_
  35.5 0.0 collective-permute-done.16.refs_8_
  35.5 0.0 copy-done.2
  35.5 0.0 copy-done.3
  35.5 1.1 %last.1 = (f32[16,256]{1,0:T(8,128)}, f32[16,512]{1,0:T(8,128)}, f32[1,16]{1,0:T(1,128)}, f32[1,16]{1,0:T(1,128)}) custom-call(bf16[48,256]{1,0:T(8,128)(2,1)S(1)} %collective-permute-done.12.refs_0_, bf16[48,256]{1,0:T(8,128)(2,1)S(1)} %collective-permute-done.13.refs_1_, bf16[48,256]{1,0:T(8,128)(2,1)S(1)} %collective-permute-done.14.refs_2_, ...), custom_call_target="tpu_custom_call" | custom-call | flops 4194304000 | bytes 8388608 | tf_op jit(solution)/shard_map/last/pallas_call | solution.py:31
  (6 shorter events, 0.1 us)
Async XLA Ops:
  1.7 5.9 %collective-permute-start = (bf16[16,640]{1,0:T(8,128)(2,1)S(1)}, bf16[16,640]{1,0:T(8,128)(2,1)S(1)}, u32[]{:S(2)}, u32[]{:S(2)}) collective-permute-start(bf16[16,640]{1,0:T(8,128)(2,1)S(1)} %prep.1.refs_3_), channel_id=1, source_target_pairs={{0,16},{1,17},{2,18},{3,19},{4,20},{5,21},{6,22},{7,23},{8,24},{9,... | collective-permute-start | bytes 61448 | tf_op jit(solution)/shard_map/ppermute | solution.py:361
  5.8 5.0 %collective-permute-start.1 = (bf16[16,640]{1,0:T(8,128)(2,1)S(1)}, bf16[16,640]{1,0:T(8,128)(2,1)S(1)}, u32[]{:S(2)}, u32[]{:S(2)}) collective-permute-start(bf16[16,640]{1,0:T(8,128)(2,1)S(1)} %prep.1.refs_3_), channel_id=1, source_target_pairs={{0,25},{1,24},{2,27},{3,26},{4,29},{5,28},{6,31},{7,30},{8,17},{9,... | collective-permute-start | bytes 61448 | tf_op jit(solution)/shard_map/ppermute | solution.py:361
  6.4 4.5 %collective-permute-start.2 = (bf16[16,640]{1,0:T(8,128)(2,1)S(1)}, bf16[16,640]{1,0:T(8,128)(2,1)S(1)}, u32[]{:S(2)}, u32[]{:S(2)}) collective-permute-start(bf16[16,640]{1,0:T(8,128)(2,1)S(1)} %prep.1.refs_3_), channel_id=1, source_target_pairs={{0,9},{1,8},{2,11},{3,10},{4,13},{5,12},{6,15},{7,14},{8,1},{9,0},... | collective-permute-start | bytes 61448 | tf_op jit(solution)/shard_map/ppermute | solution.py:361
  10.9 5.3 %collective-permute-start.3 = (bf16[144,128]{1,0:T(8,128)(2,1)S(1)}, bf16[144,128]{1,0:T(8,128)(2,1)S(1)}, u32[]{:S(2)}, u32[]{:S(2)}) collective-permute-start(bf16[144,128]{1,0:T(8,128)(2,1)S(1)} %get-tuple-element.50.refs_3_), channel_id=1, source_target_pairs={{0,6},{1,7},{2,4},{3,5},{4,2},{5,3},{6,0},{7,1},{8,14},{9,15},{10,... | collective-permute-start | bytes 110600 | tf_op jit(solution)/shard_map/ppermute | solution.py:361
  13.4 3.8 %collective-permute-start.4 = (bf16[144,128]{1,0:T(8,128)(2,1)S(1)}, bf16[144,128]{1,0:T(8,128)(2,1)S(1)}, u32[]{:S(2)}, u32[]{:S(2)}) collective-permute-start(bf16[144,128]{1,0:T(8,128)(2,1)S(1)} %get-tuple-element.50.refs_3_), channel_id=1, source_target_pairs={{0,5},{1,4},{2,7},{3,6},{4,1},{5,0},{6,3},{7,2},{8,13},{9,12},{10,... | collective-permute-start | bytes 110600 | tf_op jit(solution)/shard_map/ppermute | solution.py:361
  13.4 3.8 %collective-permute-start.5 = (bf16[144,128]{1,0:T(8,128)(2,1)S(1)}, bf16[144,128]{1,0:T(8,128)(2,1)S(1)}, u32[]{:S(2)}, u32[]{:S(2)}) collective-permute-start(bf16[144,128]{1,0:T(8,128)(2,1)S(1)} %get-tuple-element.50.refs_3_), channel_id=1, source_target_pairs={{0,3},{1,2},{2,1},{3,0},{4,7},{5,6},{6,5},{7,4},{8,11},{9,10},{10,... | collective-permute-start | bytes 110600 | tf_op jit(solution)/shard_map/ppermute | solution.py:361
  14.2 3.0 %copy-start.1 = (f32[2048,512]{1,0:T(8,128)S(1)}, f32[2048,512]{1,0:T(8,128)}, u32[]{:S(2)}) copy-start(f32[2048,512]{1,0:T(8,128)} %refs_4_.4) | copy-start | bytes 12582916
  16.2 1.3 %copy-start = (f32[16,256]{1,0:T(8,128)S(1)}, f32[16,256]{1,0:T(8,128)}, u32[]{:S(2)}) copy-start(f32[16,256]{1,0:T(8,128)} %refs_6_.1) | copy-start | bytes 49156
  17.2 1.6 %collective-permute-start.6 = (bf16[576,128]{1,0:T(8,128)(2,1)S(1)}, bf16[576,128]{1,0:T(8,128)(2,1)S(1)}, u32[]{:S(2)}, u32[]{:S(2)}) collective-permute-start(bf16[576,128]{1,0:T(8,128)(2,1)S(1)} %join.3.refs_0_), channel_id=1, source_target_pairs={{0,1},{1,0},{2,3},{3,2},{4,5},{5,4},{6,7},{7,6},{8,9},{9,8},{10,11... | collective-permute-start | bytes 442376 | tf_op jit(solution)/shard_map/ppermute | solution.py:361
  17.5 4.3 %collective-permute-start.7 = (bf16[64,256]{1,0:T(8,128)(2,1)S(1)}, bf16[64,256]{1,0:T(8,128)(2,1)S(1)}, u32[]{:S(2)}, u32[]{:S(2)}) collective-permute-start(bf16[64,256]{1,0:T(8,128)(2,1)S(1)} %get-tuple-element.59.refs_1_), channel_id=1, source_target_pairs={{0,5},{1,4},{2,7},{3,6},{4,1},{5,0},{6,3},{7,2},{8,13},{9,12},{10,... | collective-permute-start | bytes 98312 | tf_op jit(solution)/shard_map/ppermute | solution.py:361
  21.9 0.7 %copy-start.4 = (f32[256]{0:T(256)S(1)}, f32[256]{0:T(256)}, u32[]{:S(2)}) copy-start(f32[256]{0:T(256)} %param.21) | copy-start | bytes 3076
  21.9 0.7 %copy-start.5 = (f32[256]{0:T(256)S(1)}, f32[256]{0:T(256)}, u32[]{:S(2)}) copy-start(f32[256]{0:T(256)} %param.20) | copy-start | bytes 3076
  21.9 1.5 %collective-permute-start.8 = (bf16[288,256]{1,0:T(8,128)(2,1)S(1)}, bf16[288,256]{1,0:T(8,128)(2,1)S(1)}, u32[]{:S(2)}, u32[]{:S(2)}) collective-permute-start(bf16[288,256]{1,0:T(8,128)(2,1)S(1)} %get-tuple-element.60), channel_id=1, source_target_pairs={{0,1},{1,0},{2,3},{3,2},{4,5},{5,4},{6,7},{7,6},{8,9},{9,8},{10,11... | collective-permute-start | bytes 442376 | tf_op jit(solution)/shard_map/ppermute | solution.py:361
  23.4 5.6 %collective-permute-start.10 = (bf16[96,256]{1,0:T(8,128)(2,1)S(1)}, bf16[96,256]{1,0:T(8,128)(2,1)S(1)}, u32[]{:S(2)}, u32[]{:S(2)}) collective-permute-start(bf16[96,256]{1,0:T(8,128)(2,1)S(1)} %get-tuple-element.68), channel_id=1, source_target_pairs={{0,6},{1,7},{2,4},{3,5},{4,2},{5,3},{6,0},{7,1},{8,14},{9,15},{10,... | collective-permute-start | bytes 147464 | tf_op jit(solution)/shard_map/ppermute | solution.py:361
  25.6 4.0 %collective-permute-start.11 = (bf16[96,256]{1,0:T(8,128)(2,1)S(1)}, bf16[96,256]{1,0:T(8,128)(2,1)S(1)}, u32[]{:S(2)}, u32[]{:S(2)}) collective-permute-start(bf16[96,256]{1,0:T(8,128)(2,1)S(1)} %get-tuple-element.69), channel_id=1, source_target_pairs={{0,5},{1,4},{2,7},{3,6},{4,1},{5,0},{6,3},{7,2},{8,13},{9,12},{10,... | collective-permute-start | bytes 147464 | tf_op jit(solution)/shard_map/ppermute | solution.py:361
  25.9 3.7 %collective-permute-start.9 = (bf16[96,256]{1,0:T(8,128)(2,1)S(1)}, bf16[96,256]{1,0:T(8,128)(2,1)S(1)}, u32[]{:S(2)}, u32[]{:S(2)}) collective-permute-start(bf16[96,256]{1,0:T(8,128)(2,1)S(1)} %get-tuple-element.67), channel_id=1, source_target_pairs={{0,3},{1,2},{2,1},{3,0},{4,7},{5,6},{6,5},{7,4},{8,11},{9,10},{10,... | collective-permute-start | bytes 147464 | tf_op jit(solution)/shard_map/ppermute | solution.py:361
  28.0 4.8 %collective-permute-start.15 = (bf16[128,256]{1,0:T(8,128)(2,1)S(1)}, bf16[128,256]{1,0:T(8,128)(2,1)S(1)}, u32[]{:S(2)}, u32[]{:S(2)}) collective-permute-start(bf16[128,256]{1,0:T(8,128)(2,1)S(1)} %join.4.refs_1_), channel_id=1, source_target_pairs={{0,3},{1,2},{2,1},{3,0},{4,7},{5,6},{6,5},{7,4},{8,11},{9,10},{10,... | collective-permute-start | bytes 196616 | tf_op jit(solution)/shard_map/ppermute | solution.py:361
  29.6 5.0 %collective-permute-start.12 = (bf16[48,256]{1,0:T(8,128)(2,1)S(1)}, bf16[48,256]{1,0:T(8,128)(2,1)S(1)}, u32[]{:S(2)}, u32[]{:S(2)}) collective-permute-start(bf16[48,256]{1,0:T(8,128)(2,1)S(1)} %get-tuple-element.81), channel_id=1, source_target_pairs={{0,16},{1,17},{2,18},{3,19},{4,20},{5,21},{6,22},{7,23},{8,24},{9,... | collective-permute-start | bytes 73736 | tf_op jit(solution)/shard_map/ppermute | solution.py:361
  30.4 5.1 %collective-permute-start.13 = (bf16[48,256]{1,0:T(8,128)(2,1)S(1)}, bf16[48,256]{1,0:T(8,128)(2,1)S(1)}, u32[]{:S(2)}, u32[]{:S(2)}) collective-permute-start(bf16[48,256]{1,0:T(8,128)(2,1)S(1)} %get-tuple-element.82), channel_id=1, source_target_pairs={{0,25},{1,24},{2,27},{3,26},{4,29},{5,28},{6,31},{7,30},{8,17},{9,... | collective-permute-start | bytes 73736 | tf_op jit(solution)/shard_map/ppermute | solution.py:361
  31.8 3.7 %collective-permute-start.14 = (bf16[48,256]{1,0:T(8,128)(2,1)S(1)}, bf16[48,256]{1,0:T(8,128)(2,1)S(1)}, u32[]{:S(2)}, u32[]{:S(2)}) collective-permute-start(bf16[48,256]{1,0:T(8,128)(2,1)S(1)} %get-tuple-element.83), channel_id=1, source_target_pairs={{0,9},{1,8},{2,11},{3,10},{4,13},{5,12},{6,15},{7,14},{8,1},{9,0},... | collective-permute-start | bytes 73736 | tf_op jit(solution)/shard_map/ppermute | solution.py:361
  32.9 2.6 %collective-permute-start.16 = (bf16[256,256]{1,0:T(8,128)(2,1)S(1)}, bf16[256,256]{1,0:T(8,128)(2,1)S(1)}, u32[]{:S(2)}, u32[]{:S(2)}) collective-permute-start(bf16[256,256]{1,0:T(8,128)(2,1)S(1)} %join.5.refs_7_), channel_id=1, source_target_pairs={{0,1},{1,0},{2,3},{3,2},{4,5},{5,4},{6,7},{7,6},{8,9},{9,8},{10,11... | collective-permute-start | bytes 393224 | tf_op jit(solution)/shard_map/ppermute | solution.py:361
  33.1 2.3 %copy-start.2 = (f32[16,512]{1,0:T(8,128)S(1)}, f32[16,512]{1,0:T(8,128)}, u32[]{:S(2)}) copy-start(f32[16,512]{1,0:T(8,128)} %refs_4_.5) | copy-start | bytes 98308
  33.1 2.3 %copy-start.3 = (f32[16]{0:T(128)S(1)}, f32[16]{0:T(128)}, u32[]{:S(2)}) copy-start(f32[16]{0:T(128)} %param.17) | copy-start | bytes 196

commit v2 on v0

--- a/solution.py
+++ b/solution.py
@@ -412,7 +412,7 @@
         ],
         space=pl.ANY,
     )
-    tile, layer_tile = min(512, points), min(512, points)
+    tile, layer_tile = min(256, points), min(512, points)
     x, x_t = pl.pallas_call(
         functools.partial(inputs_kernel, hid, tile),
         out_shape=[

time: 36.8 us -> 37.2 us (1.011)
  no operation moved by 1% of the time
where the time goes in v2:
time: 37.2 us; the launch traced here: 36.9 us
  starting transfers between devices  17 us (46%)
  Pallas kernels  10.1 us (27%)
  waiting for transfers between devices  8.27 us (22%)
  between operations  0.79 us (2%)
  other arithmetic  0.59 us (2%)
    ppermute x17, starting transfers between devices, swaps(): lax.ppermute(x, AXES, [(i, i ^ mask) for i in range(devices)])  17 us
    ppermute x17, waiting for transfers between devices, swaps(): lax.ppermute(x, AXES, [(i, i ^ mask) for i in range(devices)])  8.27 us
    pallas_call x1, Pallas kernels, per_device(): pl.pallas_call(functools.partial(layer_kernel, hid, shapes, layer_tile, o...  3.04 us
    pallas_call x2, Pallas kernels, store(): pl.pallas_call(body, out_shape=pltpu.HBM(shape, F32), in_specs=[pl.BlockS...  2.66 us
    pallas_call x8, Pallas kernels, small_kernel(): pl.pallas_call(body, out_shape=out_shape, in_specs=[pl.BlockSpec(memory_s...  2.35 us
    pallas_call x1, Pallas kernels, per_device(): pl.pallas_call(functools.partial(inputs_kernel, hid, tile), out_shape=[sh...  2.09 us
  transfers between devices with their start and end apart: 17, of which 9 were waited for; matrix products, arithmetic and copies ran while one was open for 2% of the time, Pallas kernels for 21%

profile of v2, /device:TPU:0, one launch (start us, length us, event | category | flops | bytes accessed | tf_op | source)
XLA Modules:
  0.0 36.9 jit_solution(7431786882258188284)
XLA Ops:
  0.6 1.1 %prep.1.refs_3_ = bf16[16,640]{1,0:T(8,128)(2,1)S(1)} custom-call(f32[16,512]{1,0:T(8,128)} %refs_4_.5, f32[1,16]{1,0:T(1,128)} %bitcast.7, f32[1,16]{1,0:T(1,128)} %bitcast.12, f32[16,256]{1,0:T(8,128)} %refs_6_.1), custom_call_target="tpu_custom_call" | custom-call | flops 4194304000 | bytes 8388608 | tf_op jit(solution)/shard_map/prep/pallas_call | solution.py:31
  1.7 4.1 %collective-permute-start = (bf16[16,640]{1,0:T(8,128)(2,1)S(1)}, bf16[16,640]{1,0:T(8,128)(2,1)S(1)}, u32[]{:S(2)}, u32[]{:S(2)}) collective-permute-start(bf16[16,640]{1,0:T(8,128)(2,1)S(1)} %prep.1.refs_3_), channel_id=1, source_target_pairs={{0,16},{1,17},{2,18},{3,19},{4,20},{5,21},{6,22},{7,23},{8,24},{9,... | collective-permute-start | bytes 61448 | tf_op jit(solution)/shard_map/ppermute | solution.py:361
  5.8 0.5 %collective-permute-start.1 = (bf16[16,640]{1,0:T(8,128)(2,1)S(1)}, bf16[16,640]{1,0:T(8,128)(2,1)S(1)}, u32[]{:S(2)}, u32[]{:S(2)}) collective-permute-start(bf16[16,640]{1,0:T(8,128)(2,1)S(1)} %prep.1.refs_3_), channel_id=1, source_target_pairs={{0,25},{1,24},{2,27},{3,26},{4,29},{5,28},{6,31},{7,30},{8,17},{9,... | collective-permute-start | bytes 61448 | tf_op jit(solution)/shard_map/ppermute | solution.py:361
  6.4 0.2 collective-permute-start.2
  6.6 2.1 %inputs.1 = (bf16[2048,384]{1,0:T(8,128)(2,1)S(1)}, bf16[272,2048]{1,0:T(8,128)(2,1)S(1)}) custom-call(f32[2048,253]{1,0:T(8,128)} %refs_0_.3, f32[3,2048]{1,0:T(4,128)} %bitcast.9, s32[1,2048]{1,0:T(1,128)} %bitcast.10, s32[1,2048]{1,0:T(1,128)} %bitcast.11), custom_call_target="tpu_custom_call" | custom-call | flops 4194304000 | bytes 4194304 | tf_op jit(solution)/shard_map/inputs/pallas_call | solution.py:416
  8.7 0.0 copy-start.1
  8.7 0.0 collective-permute-done.refs_0_
  8.7 2.2 %collective-permute-done.1.refs_1_ = bf16[16,640]{1,0:T(8,128)(2,1)S(1)} collective-permute-done((bf16[16,640]{1,0:T(8,128)(2,1)S(1)}, bf16[16,640]{1,0:T(8,128)(2,1)S(1)}, u32[]{:S(2)}, u32[]{:S(2)}) %collective-permute-start.1) | collective-permute-done | bytes 20512 | tf_op jit(solution)/shard_map/ppermute | solution.py:361
  10.9 0.0 collective-permute-done.2.refs_2_
  10.9 0.1 pack.1
  10.9 0.0 copy-start
  10.9 2.5 %collective-permute-start.3 = (bf16[144,128]{1,0:T(8,128)(2,1)S(1)}, bf16[144,128]{1,0:T(8,128)(2,1)S(1)}, u32[]{:S(2)}, u32[]{:S(2)}) collective-permute-start(bf16[144,128]{1,0:T(8,128)(2,1)S(1)} %get-tuple-element.55.refs_3_), channel_id=1, source_target_pairs={{0,6},{1,7},{2,4},{3,5},{4,2},{5,3},{6,0},{7,1},{8,14},{9,15},{10,... | collective-permute-start | bytes 110600 | tf_op jit(solution)/shard_map/ppermute | solution.py:361
  13.4 0.0 collective-permute-start.4
  13.4 0.8 %collective-permute-start.5 = (bf16[144,128]{1,0:T(8,128)(2,1)S(1)}, bf16[144,128]{1,0:T(8,128)(2,1)S(1)}, u32[]{:S(2)}, u32[]{:S(2)}) collective-permute-start(bf16[144,128]{1,0:T(8,128)(2,1)S(1)} %get-tuple-element.55.refs_3_), channel_id=1, source_target_pairs={{0,3},{1,2},{2,1},{3,0},{4,7},{5,6},{6,5},{7,4},{8,11},{9,10},{10,... | collective-permute-start | bytes 110600 | tf_op jit(solution)/shard_map/ppermute | solution.py:361
  14.2 1.6 %collective-permute-done.3.refs_0_ = bf16[144,128]{1,0:T(8,128)(2,1)S(1)} collective-permute-done((bf16[144,128]{1,0:T(8,128)(2,1)S(1)}, bf16[144,128]{1,0:T(8,128)(2,1)S(1)}, u32[]{:S(2)}, u32[]{:S(2)}) %collective-permute-start.3) | collective-permute-done | bytes 36896 | tf_op jit(solution)/shard_map/ppermute | solution.py:361
  15.8 1.4 %collective-permute-done.4.refs_1_ = bf16[144,128]{1,0:T(8,128)(2,1)S(1)} collective-permute-done((bf16[144,128]{1,0:T(8,128)(2,1)S(1)}, bf16[144,128]{1,0:T(8,128)(2,1)S(1)}, u32[]{:S(2)}, u32[]{:S(2)}) %collective-permute-start.4) | collective-permute-done | bytes 36896 | tf_op jit(solution)/shard_map/ppermute | solution.py:361
  17.2 0.0 collective-permute-done.5.refs_2_
  17.2 0.0 copy-done.1
  17.2 0.3 collective-permute-start.6
  17.5 0.0 copy-done
  17.6 1.2 %collective-permute-start.7 = (bf16[64,256]{1,0:T(8,128)(2,1)S(1)}, bf16[64,256]{1,0:T(8,128)(2,1)S(1)}, u32[]{:S(2)}, u32[]{:S(2)}) collective-permute-start(bf16[64,256]{1,0:T(8,128)(2,1)S(1)} %get-tuple-element.61.refs_1_), channel_id=1, source_target_pairs={{0,5},{1,4},{2,7},{3,6},{4,1},{5,0},{6,3},{7,2},{8,13},{9,12},{10,... | collective-permute-start | bytes 98312 | tf_op jit(solution)/shard_map/ppermute | solution.py:361
  18.7 0.0 collective-permute-done.6.refs_1_
  18.7 3.0 %layer.1 = (f32[2048,512]{1,0:T(8,128)}, f32[1024,512]{1,0:T(8,128)S(1)}, f32[2048,253]{1,0:T(8,128)S(1)}, bf16[288,256]{1,0:T(8,128)(2,1)S(1)}, bf16[288,256]{1,0:T(8,128)(2,1)S(1)}) custom-call(bf16[576,128]{1,0:T(8,128)(2,1)S(1)} %join.3.refs_0_, bf16[576,128]{1,0:T(8,128)(2,1)S(1)} %collective-permute-done.6.refs_1_, ...), custom_call_target="tpu_custom_call" | custom-call | flops 3221225472 | bytes 12582912 | tf_op jit(solution)/shard_map/layer/pallas_call | solution.py:487
  21.8 0.0 collective-permute-done.7.refs_0_
  21.8 0.0 copy-start.4
  21.8 0.0 copy-start.5
  21.8 0.6 %collective-permute-start.8 = (bf16[288,256]{1,0:T(8,128)(2,1)S(1)}, bf16[288,256]{1,0:T(8,128)(2,1)S(1)}, u32[]{:S(2)}, u32[]{:S(2)}) collective-permute-start(bf16[288,256]{1,0:T(8,128)(2,1)S(1)} %get-tuple-element.62), channel_id=1, source_target_pairs={{0,1},{1,0},{2,3},{3,2},{4,5},{5,4},{6,7},{7,6},{8,9},{9,8},{10,11... | collective-permute-start | bytes 442376 | tf_op jit(solution)/shard_map/ppermute | solution.py:361
  22.4 0.1 copy-done.4
  22.5 0.0 copy-done.5
  22.5 0.6 %multiply_add_fusion = (f32[256]{0:T(256)}, f32[256]{0:T(256)}) fusion(f32[256]{0:T(256)S(1)} %get-tuple-element.95, f32[256]{0:T(256)S(1)} %get-tuple-element.94, f32[256]{0:T(256)S(1)} %copy-done.4, f32[256]{0:T(256)S(1)} %copy-done.5), kind=kLoop, calls=%fused_computation.1 | loop fusion | flops 2560 | bytes 6144 | tf_op jit(solution)/shard_map/add | solution.py:594
  23.1 0.3 collective-permute-done.8.refs_0_
  23.4 1.3 %collective-permute-start.10 = (bf16[96,256]{1,0:T(8,128)(2,1)S(1)}, bf16[96,256]{1,0:T(8,128)(2,1)S(1)}, u32[]{:S(2)}, u32[]{:S(2)}) collective-permute-start(bf16[96,256]{1,0:T(8,128)(2,1)S(1)} %get-tuple-element.70), channel_id=1, source_target_pairs={{0,6},{1,7},{2,4},{3,5},{4,2},{5,3},{6,0},{7,1},{8,14},{9,15},{10,... | collective-permute-start | bytes 147464 | tf_op jit(solution)/shard_map/ppermute | solution.py:361
  24.8 0.4 %collective-permute-start.11 = (bf16[96,256]{1,0:T(8,128)(2,1)S(1)}, bf16[96,256]{1,0:T(8,128)(2,1)S(1)}, u32[]{:S(2)}, u32[]{:S(2)}) collective-permute-start(bf16[96,256]{1,0:T(8,128)(2,1)S(1)} %get-tuple-element.71), channel_id=1, source_target_pairs={{0,5},{1,4},{2,7},{3,6},{4,1},{5,0},{6,3},{7,2},{8,13},{9,12},{10,... | collective-permute-start | bytes 147464 | tf_op jit(solution)/shard_map/ppermute | solution.py:361
  25.2 1.6 %collective-permute-start.9 = (bf16[96,256]{1,0:T(8,128)(2,1)S(1)}, bf16[96,256]{1,0:T(8,128)(2,1)S(1)}, u32[]{:S(2)}, u32[]{:S(2)}) collective-permute-start(bf16[96,256]{1,0:T(8,128)(2,1)S(1)} %get-tuple-element.69), channel_id=1, source_target_pairs={{0,3},{1,2},{2,1},{3,0},{4,7},{5,6},{6,5},{7,4},{8,11},{9,10},{10,... | collective-permute-start | bytes 147464 | tf_op jit(solution)/shard_map/ppermute | solution.py:361
  26.7 1.3 %store.1 = f32[2048,253]{1,0:T(8,128)} custom-call(f32[2048,253]{1,0:T(8,128)S(1)} %get-tuple-element.77.source_ref), custom_call_target="tpu_custom_call" | custom-call | flops 4194304000 | bytes 4145152 | tf_op jit(solution)/shard_map/store/pallas_call | solution.py:515
  28.1 0.2 collective-permute-start.15
  28.3 0.2 collective-permute-done.10.refs_1_
  28.5 0.2 collective-permute-done.11.refs_2_
  28.7 0.5 %collective-permute-done.9.refs_0_ = bf16[96,256]{1,0:T(8,128)(2,1)S(1)} collective-permute-done((bf16[96,256]{1,0:T(8,128)(2,1)S(1)}, bf16[96,256]{1,0:T(8,128)(2,1)S(1)}, u32[]{:S(2)}, u32[]{:S(2)}) %collective-permute-start.9) | collective-permute-done | bytes 49184 | tf_op jit(solution)/shard_map/ppermute | solution.py:361
  29.2 1.3 %collective-permute-start.12 = (bf16[48,256]{1,0:T(8,128)(2,1)S(1)}, bf16[48,256]{1,0:T(8,128)(2,1)S(1)}, u32[]{:S(2)}, u32[]{:S(2)}) collective-permute-start(bf16[48,256]{1,0:T(8,128)(2,1)S(1)} %get-tuple-element.83), channel_id=1, source_target_pairs={{0,16},{1,17},{2,18},{3,19},{4,20},{5,21},{6,22},{7,23},{8,24},{9,... | collective-permute-start | bytes 73736 | tf_op jit(solution)/shard_map/ppermute | solution.py:361
  30.5 0.9 %collective-permute-start.13 = (bf16[48,256]{1,0:T(8,128)(2,1)S(1)}, bf16[48,256]{1,0:T(8,128)(2,1)S(1)}, u32[]{:S(2)}, u32[]{:S(2)}) collective-permute-start(bf16[48,256]{1,0:T(8,128)(2,1)S(1)} %get-tuple-element.84), channel_id=1, source_target_pairs={{0,25},{1,24},{2,27},{3,26},{4,29},{5,28},{6,31},{7,30},{8,17},{9,... | collective-permute-start | bytes 73736 | tf_op jit(solution)/shard_map/ppermute | solution.py:361
  31.4 1.1 %collective-permute-start.14 = (bf16[48,256]{1,0:T(8,128)(2,1)S(1)}, bf16[48,256]{1,0:T(8,128)(2,1)S(1)}, u32[]{:S(2)}, u32[]{:S(2)}) collective-permute-start(bf16[48,256]{1,0:T(8,128)(2,1)S(1)} %get-tuple-element.85), channel_id=1, source_target_pairs={{0,9},{1,8},{2,11},{3,10},{4,13},{5,12},{6,15},{7,14},{8,1},{9,0},... | collective-permute-start | bytes 73736 | tf_op jit(solution)/shard_map/ppermute | solution.py:361
  32.5 0.0 collective-permute-done.15.refs_0_
  32.5 0.1 collective-permute-start.16
  32.6 0.0 copy-start.2
  32.6 0.0 copy-start.3
  32.6 1.3 %tail.1 = f32[2048,512]{1,0:T(8,128)} custom-call(f32[2048,512]{1,0:T(8,128)} %get-tuple-element.58._, f32[1024,512]{1,0:T(8,128)S(1)} %get-tuple-element.81.source_ref), custom_call_target="tpu_custom_call", output_to_operand_aliasing={{}: (0, {})} | custom-call | flops 4194304000 | bytes 4145152 | tf_op jit(solution)/shard_map/tail/pallas_call | solution.py:515
  33.9 0.1 collective-permute-done.12.refs_0_
  34.0 1.8 %collective-permute-done.13.refs_1_ = bf16[48,256]{1,0:T(8,128)(2,1)S(1)} collective-permute-done((bf16[48,256]{1,0:T(8,128)(2,1)S(1)}, bf16[48,256]{1,0:T(8,128)(2,1)S(1)}, u32[]{:S(2)}, u32[]{:S(2)}) %collective-permute-start.13) | collective-permute-done | bytes 24608 | tf_op jit(solution)/shard_map/ppermute | solution.py:361
  35.8 0.0 collective-permute-done.14.refs_2_
  35.8 0.0 collective-permute-done.16.refs_8_
  35.8 0.0 copy-done.2
  35.8 0.0 copy-done.3
  35.9 1.1 %last.1 = (f32[16,256]{1,0:T(8,128)}, f32[16,512]{1,0:T(8,128)}, f32[1,16]{1,0:T(1,128)}, f32[1,16]{1,0:T(1,128)}) custom-call(bf16[48,256]{1,0:T(8,128)(2,1)S(1)} %collective-permute-done.12.refs_0_, bf16[48,256]{1,0:T(8,128)(2,1)S(1)} %collective-permute-done.13.refs_1_, bf16[48,256]{1,0:T(8,128)(2,1)S(1)} %collective-permute-done.14.refs_2_, ...), custom_call_target="tpu_custom_call" | custom-call | flops 4194304000 | bytes 8388608 | tf_op jit(solution)/shard_map/last/pallas_call | solution.py:31
  (6 shorter events, 0.1 us)
Async XLA Ops:
  1.7 7.0 %collective-permute-start = (bf16[16,640]{1,0:T(8,128)(2,1)S(1)}, bf16[16,640]{1,0:T(8,128)(2,1)S(1)}, u32[]{:S(2)}, u32[]{:S(2)}) collective-permute-start(bf16[16,640]{1,0:T(8,128)(2,1)S(1)} %prep.1.refs_3_), channel_id=1, source_target_pairs={{0,16},{1,17},{2,18},{3,19},{4,20},{5,21},{6,22},{7,23},{8,24},{9,... | collective-permute-start | bytes 61448 | tf_op jit(solution)/shard_map/ppermute | solution.py:361
  5.8 5.0 %collective-permute-start.1 = (bf16[16,640]{1,0:T(8,128)(2,1)S(1)}, bf16[16,640]{1,0:T(8,128)(2,1)S(1)}, u32[]{:S(2)}, u32[]{:S(2)}) collective-permute-start(bf16[16,640]{1,0:T(8,128)(2,1)S(1)} %prep.1.refs_3_), channel_id=1, source_target_pairs={{0,25},{1,24},{2,27},{3,26},{4,29},{5,28},{6,31},{7,30},{8,17},{9,... | collective-permute-start | bytes 61448 | tf_op jit(solution)/shard_map/ppermute | solution.py:361
  6.4 4.5 %collective-permute-start.2 = (bf16[16,640]{1,0:T(8,128)(2,1)S(1)}, bf16[16,640]{1,0:T(8,128)(2,1)S(1)}, u32[]{:S(2)}, u32[]{:S(2)}) collective-permute-start(bf16[16,640]{1,0:T(8,128)(2,1)S(1)} %prep.1.refs_3_), channel_id=1, source_target_pairs={{0,9},{1,8},{2,11},{3,10},{4,13},{5,12},{6,15},{7,14},{8,1},{9,0},... | collective-permute-start | bytes 61448 | tf_op jit(solution)/shard_map/ppermute | solution.py:361
  8.7 8.5 %copy-start.1 = (f32[2048,512]{1,0:T(8,128)S(1)}, f32[2048,512]{1,0:T(8,128)}, u32[]{:S(2)}) copy-start(f32[2048,512]{1,0:T(8,128)} %refs_4_.4) | copy-start | bytes 12582916
  10.9 6.6 %copy-start = (f32[16,256]{1,0:T(8,128)S(1)}, f32[16,256]{1,0:T(8,128)}, u32[]{:S(2)}) copy-start(f32[16,256]{1,0:T(8,128)} %refs_6_.1) | copy-start | bytes 49156
  10.9 4.9 %collective-permute-start.3 = (bf16[144,128]{1,0:T(8,128)(2,1)S(1)}, bf16[144,128]{1,0:T(8,128)(2,1)S(1)}, u32[]{:S(2)}, u32[]{:S(2)}) collective-permute-start(bf16[144,128]{1,0:T(8,128)(2,1)S(1)} %get-tuple-element.55.refs_3_), channel_id=1, source_target_pairs={{0,6},{1,7},{2,4},{3,5},{4,2},{5,3},{6,0},{7,1},{8,14},{9,15},{10,... | collective-permute-start | bytes 110600 | tf_op jit(solution)/shard_map/ppermute | solution.py:361
  13.4 3.8 %collective-permute-start.4 = (bf16[144,128]{1,0:T(8,128)(2,1)S(1)}, bf16[144,128]{1,0:T(8,128)(2,1)S(1)}, u32[]{:S(2)}, u32[]{:S(2)}) collective-permute-start(bf16[144,128]{1,0:T(8,128)(2,1)S(1)} %get-tuple-element.55.refs_3_), channel_id=1, source_target_pairs={{0,5},{1,4},{2,7},{3,6},{4,1},{5,0},{6,3},{7,2},{8,13},{9,12},{10,... | collective-permute-start | bytes 110600 | tf_op jit(solution)/shard_map/ppermute | solution.py:361
  13.4 3.8 %collective-permute-start.5 = (bf16[144,128]{1,0:T(8,128)(2,1)S(1)}, bf16[144,128]{1,0:T(8,128)(2,1)S(1)}, u32[]{:S(2)}, u32[]{:S(2)}) collective-permute-start(bf16[144,128]{1,0:T(8,128)(2,1)S(1)} %get-tuple-element.55.refs_3_), channel_id=1, source_target_pairs={{0,3},{1,2},{2,1},{3,0},{4,7},{5,6},{6,5},{7,4},{8,11},{9,10},{10,... | collective-permute-start | bytes 110600 | tf_op jit(solution)/shard_map/ppermute | solution.py:361
  17.2 1.5 %collective-permute-start.6 = (bf16[576,128]{1,0:T(8,128)(2,1)S(1)}, bf16[576,128]{1,0:T(8,128)(2,1)S(1)}, u32[]{:S(2)}, u32[]{:S(2)}) collective-permute-start(bf16[576,128]{1,0:T(8,128)(2,1)S(1)} %join.3.refs_0_), channel_id=1, source_target_pairs={{0,1},{1,0},{2,3},{3,2},{4,5},{5,4},{6,7},{7,6},{8,9},{9,8},{10,11... | collective-permute-start | bytes 442376 | tf_op jit(solution)/shard_map/ppermute | solution.py:361
  17.6 4.2 %collective-permute-start.7 = (bf16[64,256]{1,0:T(8,128)(2,1)S(1)}, bf16[64,256]{1,0:T(8,128)(2,1)S(1)}, u32[]{:S(2)}, u32[]{:S(2)}) collective-permute-start(bf16[64,256]{1,0:T(8,128)(2,1)S(1)} %get-tuple-element.61.refs_1_), channel_id=1, source_target_pairs={{0,5},{1,4},{2,7},{3,6},{4,1},{5,0},{6,3},{7,2},{8,13},{9,12},{10,... | collective-permute-start | bytes 98312 | tf_op jit(solution)/shard_map/ppermute | solution.py:361
  21.8 0.7 %copy-start.4 = (f32[256]{0:T(256)S(1)}, f32[256]{0:T(256)}, u32[]{:S(2)}) copy-start(f32[256]{0:T(256)} %param.21) | copy-start | bytes 3076
  21.8 0.7 %copy-start.5 = (f32[256]{0:T(256)S(1)}, f32[256]{0:T(256)}, u32[]{:S(2)}) copy-start(f32[256]{0:T(256)} %param.20) | copy-start | bytes 3076
  21.8 1.6 %collective-permute-start.8 = (bf16[288,256]{1,0:T(8,128)(2,1)S(1)}, bf16[288,256]{1,0:T(8,128)(2,1)S(1)}, u32[]{:S(2)}, u32[]{:S(2)}) collective-permute-start(bf16[288,256]{1,0:T(8,128)(2,1)S(1)} %get-tuple-element.62), channel_id=1, source_target_pairs={{0,1},{1,0},{2,3},{3,2},{4,5},{5,4},{6,7},{7,6},{8,9},{9,8},{10,11... | collective-permute-start | bytes 442376 | tf_op jit(solution)/shard_map/ppermute | solution.py:361
  23.4 5.1 %collective-permute-start.10 = (bf16[96,256]{1,0:T(8,128)(2,1)S(1)}, bf16[96,256]{1,0:T(8,128)(2,1)S(1)}, u32[]{:S(2)}, u32[]{:S(2)}) collective-permute-start(bf16[96,256]{1,0:T(8,128)(2,1)S(1)} %get-tuple-element.70), channel_id=1, source_target_pairs={{0,6},{1,7},{2,4},{3,5},{4,2},{5,3},{6,0},{7,1},{8,14},{9,15},{10,... | collective-permute-start | bytes 147464 | tf_op jit(solution)/shard_map/ppermute | solution.py:361
  24.8 3.9 %collective-permute-start.11 = (bf16[96,256]{1,0:T(8,128)(2,1)S(1)}, bf16[96,256]{1,0:T(8,128)(2,1)S(1)}, u32[]{:S(2)}, u32[]{:S(2)}) collective-permute-start(bf16[96,256]{1,0:T(8,128)(2,1)S(1)} %get-tuple-element.71), channel_id=1, source_target_pairs={{0,5},{1,4},{2,7},{3,6},{4,1},{5,0},{6,3},{7,2},{8,13},{9,12},{10,... | collective-permute-start | bytes 147464 | tf_op jit(solution)/shard_map/ppermute | solution.py:361
  25.2 4.0 %collective-permute-start.9 = (bf16[96,256]{1,0:T(8,128)(2,1)S(1)}, bf16[96,256]{1,0:T(8,128)(2,1)S(1)}, u32[]{:S(2)}, u32[]{:S(2)}) collective-permute-start(bf16[96,256]{1,0:T(8,128)(2,1)S(1)} %get-tuple-element.69), channel_id=1, source_target_pairs={{0,3},{1,2},{2,1},{3,0},{4,7},{5,6},{6,5},{7,4},{8,11},{9,10},{10,... | collective-permute-start | bytes 147464 | tf_op jit(solution)/shard_map/ppermute | solution.py:361
  28.1 4.4 %collective-permute-start.15 = (bf16[128,256]{1,0:T(8,128)(2,1)S(1)}, bf16[128,256]{1,0:T(8,128)(2,1)S(1)}, u32[]{:S(2)}, u32[]{:S(2)}) collective-permute-start(bf16[128,256]{1,0:T(8,128)(2,1)S(1)} %join.4.refs_1_), channel_id=1, source_target_pairs={{0,3},{1,2},{2,1},{3,0},{4,7},{5,6},{6,5},{7,4},{8,11},{9,10},{10,... | collective-permute-start | bytes 196616 | tf_op jit(solution)/shard_map/ppermute | solution.py:361
  29.2 4.8 %collective-permute-start.12 = (bf16[48,256]{1,0:T(8,128)(2,1)S(1)}, bf16[48,256]{1,0:T(8,128)(2,1)S(1)}, u32[]{:S(2)}, u32[]{:S(2)}) collective-permute-start(bf16[48,256]{1,0:T(8,128)(2,1)S(1)} %get-tuple-element.83), channel_id=1, source_target_pairs={{0,16},{1,17},{2,18},{3,19},{4,20},{5,21},{6,22},{7,23},{8,24},{9,... | collective-permute-start | bytes 73736 | tf_op jit(solution)/shard_map/ppermute | solution.py:361
  30.5 5.3 %collective-permute-start.13 = (bf16[48,256]{1,0:T(8,128)(2,1)S(1)}, bf16[48,256]{1,0:T(8,128)(2,1)S(1)}, u32[]{:S(2)}, u32[]{:S(2)}) collective-permute-start(bf16[48,256]{1,0:T(8,128)(2,1)S(1)} %get-tuple-element.84), channel_id=1, source_target_pairs={{0,25},{1,24},{2,27},{3,26},{4,29},{5,28},{6,31},{7,30},{8,17},{9,... | collective-permute-start | bytes 73736 | tf_op jit(solution)/shard_map/ppermute | solution.py:361
  31.4 4.5 %collective-permute-start.14 = (bf16[48,256]{1,0:T(8,128)(2,1)S(1)}, bf16[48,256]{1,0:T(8,128)(2,1)S(1)}, u32[]{:S(2)}, u32[]{:S(2)}) collective-permute-start(bf16[48,256]{1,0:T(8,128)(2,1)S(1)} %get-tuple-element.85), channel_id=1, source_target_pairs={{0,9},{1,8},{2,11},{3,10},{4,13},{5,12},{6,15},{7,14},{8,1},{9,0},... | collective-permute-start | bytes 73736 | tf_op jit(solution)/shard_map/ppermute | solution.py:361
  32.5 3.3 %collective-permute-start.16 = (bf16[256,256]{1,0:T(8,128)(2,1)S(1)}, bf16[256,256]{1,0:T(8,128)(2,1)S(1)}, u32[]{:S(2)}, u32[]{:S(2)}) collective-permute-start(bf16[256,256]{1,0:T(8,128)(2,1)S(1)} %join.5.refs_7_), channel_id=1, source_target_pairs={{0,1},{1,0},{2,3},{3,2},{4,5},{5,4},{6,7},{7,6},{8,9},{9,8},{10,11... | collective-permute-start | bytes 393224 | tf_op jit(solution)/shard_map/ppermute | solution.py:361
  32.6 3.3 %copy-start.2 = (f32[16,512]{1,0:T(8,128)S(1)}, f32[16,512]{1,0:T(8,128)}, u32[]{:S(2)}) copy-start(f32[16,512]{1,0:T(8,128)} %refs_4_.5) | copy-start | bytes 98308
  32.6 3.2 %copy-start.3 = (f32[16]{0:T(128)S(1)}, f32[16]{0:T(128)}, u32[]{:S(2)}) copy-start(f32[16]{0:T(128)} %param.17) | copy-start | bytes 196
